TPU v7x, 32 devices: a whole 2x2x4 slice. The times are simulated.
32 devices in a mesh: groups: 2 (over y), cells: 4 (over z), role: 2 (over x), stack: 2 (over core).
Axes of the slice: x: 2, y: 2, z: 4, core: 2. Of those that a mesh axis runs over, the one named last changes fastest.
Arguments:
- height: float32 [90, 49152], P('stack', ('groups', 'cells', 'role')), parts along dimension 1, may hold values from -6 to 6
- velocity: float32 [90, 73728], P('stack', ('groups', 'cells', 'role')), parts along dimension 1, may hold values from -6 to 6
- tracers: bfloat16 [6, 90, 49152], P(None, 'stack', ('groups', 'cells', 'role')), parts along dimension 2, may hold values from -6 to 6
- edge_coef: float32 [36864], P(('cells', 'role')), may hold values from 0.1 to 0.6
- cell_coef: float32 [3, 24576], P(None, ('cells', 'role')), may hold values from -2.5 to 2.5
- halo_send: int32 [8, 512], P(('cells', 'role')), may hold values from 0 to 3071
- edge_cells: int32 [8, 2, 4608], P(('cells', 'role')), may hold values from 0 to 3583
- cell_edges: int32 [8, 3, 3072], P(('cells', 'role')), may hold values from 0 to 4607
- send_block: int32 [8, 16], P(('cells', 'role')), may hold values from -1 to 23, as said below
- recv_slot: int32 [8, 8], P(('cells', 'role')), may hold values from 0 to 15, as said below
- block_count: int32 [8, 24], P(('cells', 'role')), may hold values from 1 to 128
- w_first: bfloat16 [900, 512], P('stack'), may hold values from -0.1875 to 0.1875
- b_first: bfloat16 [512], replicated, may hold values from -3 to 3
- w_second: bfloat16 [512, 512], P(None, 'stack'), may hold values from -0.25 to 0.25
- b_second: bfloat16 [512], P('stack'), may hold values from -3 to 3
- w_third: bfloat16 [512, 90], P('stack'), may hold values from -0.25 to 0.25
Outputs:
- height_out: float32 [90, 49152], P('stack', ('groups', 'cells', 'role')), parts along dimension 1
There are 2 independent parts, one for each index of `groups`. A program takes and returns all parts, laid end to end along the dimension named above; an argument that names none is the same for every part. Nothing has to cross between parts.
Inputs may be any that keep to these rules, and one draw needn't show every extreme that they name: `send_block`: entries are blocks of the domain or -1. Slots c * 4 to c * 4 + 3 go to the domain with cells index c and the same role index. A domain names each block at most once and fills 1 to 16 slots; in every group of domains with one role index, one domain fills exactly 16. `recv_slot`: every domain computes the physics of exactly 8 blocks; entry s names the incoming slot (s // 4 is the sender's cells index), and the sender's slot it names is filled. The entries of one domain are distinct.
All inputs are finite; a program needn't handle non-finite values.
Results may differ from a plain program's by a relative error of at most 0.0012.
Values may be sent and summed in bfloat16 or wider, within the bound.
A program may use at most 64 MiB of HBM per device.

v0:
```python
import jax
import jax.numpy as jnp
from jax import lax
from jax.sharding import PartitionSpec as P

BLK = 128


def with_halo(shard, sides, width):
    for axis, dim in sides:
        size, length = (lax.axis_size(axis), shard.shape[dim])
        up = [(i, (i + 1) % size) for i in range(size)]
        down = [(j, i) for i, j in up]
        last = lax.slice_in_dim(shard, length - width, length, axis=dim)
        first = lax.slice_in_dim(shard, 0, width, axis=dim)
        before = lax.ppermute(last, axis, up)
        after = lax.ppermute(first, axis, down)
        shard = jnp.concatenate([before, shard, after], axis=dim)
    return shard


def substep(height_rows, velocity_rows, edge_coef, cell_coef, halo_send, edge_cells, cell_edges):
    margin = halo_send.shape[1] // 2
    ncells = height_rows.shape[0]
    nedges = velocity_rows.shape[0]
    packed = jnp.take(height_rows, halo_send[0], axis=0, mode="clip")
    rims = with_halo(packed.astype(jnp.bfloat16), ((("cells", "role"), 0),), margin).astype(
        packed.dtype
    )
    extended = jnp.concatenate([height_rows, rims[:margin], rims[3 * margin :]], axis=0)
    both = jnp.take(extended, edge_cells[0].reshape(-1), axis=0, mode="clip").reshape(2, nedges, -1)
    moved = velocity_rows - edge_coef[:, None] * (both[1] - both[0])
    beside_all = jnp.take(moved, cell_edges[0].reshape(-1), axis=0, mode="clip").reshape(
        3, ncells, -1
    )
    spread = (
        cell_coef[0][:, None] * beside_all[0]
        + cell_coef[1][:, None] * beside_all[1]
        + cell_coef[2][:, None] * beside_all[2]
    )
    return (height_rows - spread, moved, spread, beside_all)


def body(
    height,
    velocity,
    tracers,
    edge_coef,
    cell_coef,
    halo_send,
    edge_cells,
    cell_edges,
    send_block,
    recv_slot,
    block_count,
    w_first,
    b_first,
    w_second,
    b_second,
    w_third,
):
    levels = height.shape[0]
    ncells = height.shape[1]
    blocks = ncells // BLK
    slots = send_block.shape[1]
    height_rows = height.T
    velocity_rows = velocity.T
    first_h, first_v, first_div, beside_all = substep(
        height_rows, velocity_rows, edge_coef, cell_coef, halo_send, edge_cells, cell_edges
    )
    derived = (
        jnp.stack(
            [
                first_h,
                first_div,
                jnp.mean(beside_all * beside_all, axis=0),
                jnp.mean(beside_all, axis=0),
            ]
        )
        .astype(jnp.bfloat16)
        .transpose(0, 2, 1)
    )
    quantities = jnp.concatenate([derived, tracers], axis=0)
    nquant = quantities.shape[0]
    features = (
        quantities.reshape(nquant, levels, blocks, BLK)
        .transpose(2, 1, 0, 3)
        .reshape(blocks, levels * nquant, BLK)
    )
    chooser = (send_block[0][:, None] == jnp.arange(blocks, dtype=jnp.int32)[None, :]).astype(
        jnp.bfloat16
    )
    outgoing = jnp.einsum(
        "sb,bfi->sfi", chooser, features, preferred_element_type=jnp.float32
    ).astype(jnp.bfloat16)
    arrived = lax.all_to_all(outgoing, "cells", split_axis=0, concat_axis=0, tiled=True)
    second_h, second_v, second_div, second_around = substep(
        first_h, first_v, edge_coef, cell_coef, halo_send, edge_cells, cell_edges
    )
    picked = jnp.take(arrived, recv_slot[0], axis=0)
    partial_one = jnp.einsum("nfi,fh->nhi", picked, w_first, preferred_element_type=jnp.float32)
    summed_one = lax.psum(partial_one, "stack")
    act_one = jax.nn.silu(summed_one + b_first.astype(jnp.float32)[None, :, None]).astype(
        jnp.bfloat16
    )
    pre_two = jnp.einsum("nhi,hk->nki", act_one, w_second, preferred_element_type=jnp.float32)
    act_two = jax.nn.silu(pre_two + b_second.astype(jnp.float32)[None, :, None]).astype(
        jnp.bfloat16
    )
    terms = jnp.einsum("nki,kl->nli", act_two, w_third, preferred_element_type=jnp.float32)
    tendency = lax.psum_scatter(terms, "stack", scatter_dimension=1, tiled=True).astype(
        jnp.bfloat16
    )
    placer = (recv_slot[0][:, None] == jnp.arange(slots, dtype=jnp.int32)[None, :]).astype(
        jnp.bfloat16
    )
    outbound = jnp.einsum(
        "rs,rli->sli", placer, tendency, preferred_element_type=jnp.float32
    ).astype(jnp.bfloat16)
    returned = lax.all_to_all(outbound, "cells", split_axis=0, concat_axis=0, tiled=True)
    block_tend = jnp.einsum("sb,sli->bli", chooser, returned, preferred_element_type=jnp.float32)
    live = (jnp.arange(BLK, dtype=jnp.int32)[None, :] < block_count[0][:, None]).astype(jnp.float32)
    block_tend = block_tend * live[:, None, :]
    added = block_tend.transpose(1, 0, 2).reshape(levels, ncells)
    return second_h.T + added


def solution(mesh):
    placed = (
        P("stack", ("groups", "cells", "role")),
        P("stack", ("groups", "cells", "role")),
        P(None, "stack", ("groups", "cells", "role")),
        P(("cells", "role")),
        P(None, ("cells", "role")),
        P(("cells", "role"), None),
        P(("cells", "role"), None, None),
        P(("cells", "role"), None, None),
        P(("cells", "role"), None),
        P(("cells", "role"), None),
        P(("cells", "role"), None),
        P("stack", None),
        P(),
        P(None, "stack"),
        P("stack"),
        P("stack", None),
    )
    return jax.shard_map(
        body,
        mesh=mesh,
        in_specs=placed,
        out_specs=P("stack", ("groups", "cells", "role")),
        check_vma=False,
    )
```

profile of v0, /device:TPU:0, one launch (start us, length us, event | category | flops | bytes accessed | tf_op | source)
XLA Modules:
  0.0 280.9 jit_solution(10388421713023140337)
XLA Ops:
  6.5 1.6 copy.162
  10.3 6.0 %collective-permute-start.1 = (bf16[256,45]{0,1:T(8,128)(2,1)S(1)}, bf16[256,45]{0,1:T(8,128)(2,1)S(1)}, u32[]{:S(2)}, u32[]{:S(2)}) collective-permute-start(bf16[256,45]{0,1:T(8,128)(2,1)S(1)} %get-tuple-element.26), channel_id=1, source_target_pairs={{2,0},{4,2},{6,4},{8,6},{10,8},{12,10},{14,12},{0,14},{3,1},{5,3},... | collective-permute-start | bytes 69128 | tf_op jit(solution)/shard_map/ppermute | solution.py:17
  16.4 1.9 copy.161
  18.4 4.4 %collective-permute-done = bf16[256,45]{0,1:T(8,128)(2,1)S(1)} collective-permute-done((bf16[256,45]{0,1:T(8,128)(2,1)S(1)}, bf16[256,45]{0,1:T(8,128)(2,1)S(1)}, u32[]{:S(2)}, u32[]{:S(2)}) %collective-permute-start) | collective-permute-done | bytes 23072 | tf_op jit(solution)/shard_map/ppermute | solution.py:16
  23.8 1.7 copy.164
  25.4 31.0 %gather_fusion.1 = f32[9216,45]{1,0:T(8,128)} fusion(f32[3584,45]{1,0:T(8,128)S(1)} %copy.164, s32[9216]{0:T(1024)S(1)} %broadcast_clamp_fusion.1), kind=kCustom, calls=%fused_computation.1 | custom fusion | bytes 3354624 | tf_op jit(solution)/shard_map/jit(_take)/gather | solution.py:31
  56.5 4.0 %fusion.3 = f32[4608,45]{1,0:T(8,128)S(1)} fusion(f32[9216,45]{1,0:T(8,128)} %gather_fusion.1, f32[45,4608]{0,1:T(8,128)} %copy.161, f32[4608]{0:T(1024)S(1)} %copy-done.14), kind=kLoop, calls=%fused_computation.14 | loop fusion | flops 622080 | bytes 3336192 | tf_op jit(solution)/shard_map/sub | solution.py:32
  60.5 31.2 %gather_fusion.2 = f32[9216,45]{1,0:T(8,128)} fusion(f32[4608,45]{1,0:T(8,128)S(1)} %fusion.3, s32[9216]{0:T(1024)S(1)} %broadcast_clamp_fusion), kind=kCustom, calls=%fused_computation.2 | custom fusion | bytes 3354624 | tf_op jit(solution)/shard_map/jit(_take)/gather | solution.py:33
  91.7 4.7 %fusion.35 = (f32[3072,45]{1,0:T(8,128)}, f32[3072,45]{1,0:T(8,128)}, f32[3072,45]{1,0:T(8,128)}) fusion(f32[9216,45]{1,0:T(8,128)} %gather_fusion.2), kind=kLoop, calls=%fused_computation.75 | loop fusion | bytes 3317760 | tf_op jit(solution)/shard_map/slice | solution.py:37
  100.8 2.0 copy.191
  102.8 2.7 copy.190
  106.8 2.4 convert_bitcast_fusion.1
  110.2 2.7 maximum_bitcast_fusion
  113.6 3.4 %reshape.149 = bf16[10,45,24,128]{3,2,1,0:T(8,128)(2,1)} reshape(bf16[10,45,3072]{2,1,0:T(8,128)(2,1)S(1)} %pad_maximum_fusion) | data formatting | bytes 5529600 | tf_op jit(solution)/shard_map/reshape | solution.py:86
  117.0 2.3 copy.180
  120.1 1.7 copy.181
  121.8 3.7 %all-to-all-start = ((bf16[16,450,128]{2,1,0:T(8,128)(2,1)}), bf16[16,450,128]{2,1,0:T(8,128)(2,1)S(1)}, u32[]{:S(2)}, u32[]{:S(2)}) async-start(bf16[16,450,128]{2,1,0:T(8,128)(2,1)} %copy.181), calls=%async_computation | async-start | bytes 3735552 | tf_op jit(solution)/shard_map/all_to_all | solution.py:96
  125.8 41.8 %all-to-all-done = bf16[16,450,128]{2,1,0:T(8,128)(2,1)S(1)} async-done(((bf16[16,450,128]{2,1,0:T(8,128)(2,1)}), bf16[16,450,128]{2,1,0:T(8,128)(2,1)S(1)}, u32[]{:S(2)}, u32[]{:S(2)}) %all-to-all-start) | async-done | bytes 1843232 | tf_op jit(solution)/shard_map/all_to_all | solution.py:96
  167.6 1.6 gather_fusion.6
  169.2 3.6 %convolution_bitcast_fusion = f32[8,512,128]{1,2,0:T(8,128)} fusion(bf16[8,450,128]{2,1,0:T(8,128)(2,1)} %gather_fusion.6, pred[8]{0:T(512)(128)(4,1)S(1)} %compare_and_fusion, bf16[450,512]{1,0:T(8,128)(2,1)S(1)} %copy-done), kind=kOutput, calls=%fused_computation.17 | convolution fusion | flops 472320000 | bytes 3479560 | tf_op jit(solution)/shard_map/nfi,fh->nhi/dot_general | solution.py:101
  174.9 2.0 collective-permute-start.2
  177.0 1.7 collective-permute-done.3
  178.7 2.8 collective-permute-done.2
  182.4 1.7 copy.170
  184.1 31.0 %gather_fusion.4 = f32[9216,45]{1,0:T(8,128)} fusion(f32[3584,45]{1,0:T(8,128)S(1)} %copy.170, s32[9216]{0:T(1024)S(1)} %broadcast_clamp_fusion.1), kind=kCustom, calls=%fused_computation.4 | custom fusion | bytes 3354624 | tf_op jit(solution)/shard_map/jit(_take)/gather | solution.py:31
  215.1 2.7 convolution_bitcast_fusion.1
  218.8 4.6 %fusion.1 = f32[4608,45]{1,0:T(8,128)} fusion(f32[4608,45]{1,0:T(8,128)S(1)} %copy-done.3, f32[9216,45]{1,0:T(8,128)} %gather_fusion.4, f32[4608]{0:T(1024)S(1)} %copy-done.14), kind=kLoop, calls=%fused_computation.11 | loop fusion | flops 622080 | bytes 3336192 | tf_op jit(solution)/shard_map/sub | solution.py:32
  223.5 32.7 %gather_fusion.5 = f32[9216,45]{1,0:T(8,128)} fusion(f32[4608,45]{1,0:T(8,128)} %fusion.1, s32[9216]{0:T(1024)S(1)} %broadcast_clamp_fusion), kind=kCustom, calls=%fused_computation.5 | custom fusion | bytes 3354624 | tf_op jit(solution)/shard_map/jit(_take)/gather | solution.py:33
  258.2 3.4 %all-to-all-start.1 = ((bf16[16,45,128]{2,1,0:T(8,128)(2,1)}), bf16[16,45,128]{2,1,0:T(8,128)(2,1)S(1)}, u32[]{:S(2)}, u32[]{:S(2)}) async-start(bf16[16,45,128]{2,1,0:T(8,128)(2,1)} %copy.184), calls=%async_computation.1 | async-start | bytes 393216 | tf_op jit(solution)/shard_map/all_to_all | solution.py:120
  261.5 4.3 %fusion.34 = (f32[3072,45]{1,0:T(8,128)S(1)}, f32[3072,45]{1,0:T(8,128)}, f32[3072,45]{1,0:T(8,128)}) fusion(f32[9216,45]{1,0:T(8,128)} %gather_fusion.5), kind=kLoop, calls=%fused_computation.74 | loop fusion | bytes 3317760 | tf_op jit(solution)/shard_map/slice | solution.py:37
  265.9 1.9 copy.194
  267.8 2.7 copy.193
  (100 shorter events, 20.9 us)
Async XLA Ops:
  6.5 162.7 %copy-start = (bf16[450,512]{1,0:T(8,128)(2,1)S(1)}, bf16[450,512]{1,0:T(8,128)(2,1)}, u32[]{:S(2)}) copy-start(bf16[450,512]{1,0:T(8,128)(2,1)} %param.27) | copy-start | bytes 1382404
  6.5 9.8 %copy-start.15 = (s32[1,2,4608]{2,1,0:T(2,128)S(1)}, s32[1,2,4608]{2,1,0:T(2,128)}, u32[]{:S(2)}) copy-start(s32[1,2,4608]{2,1,0:T(2,128)} %param.22) | copy-start | bytes 110596
  6.5 9.8 %copy-start.17 = (f32[3,3072]{1,0:T(4,128)S(1)}, f32[3,3072]{1,0:T(4,128)}, u32[]{:S(2)}) copy-start(f32[3,3072]{1,0:T(4,128)} %param.20) | copy-start | bytes 110596
  6.5 9.9 %copy-start.16 = (s32[1,3,3072]{2,0,1:T(1,128)S(1)}, s32[1,3,3072]{2,0,1:T(1,128)}, u32[]{:S(2)}) copy-start(s32[1,3,3072]{2,0,1:T(1,128)} %param.23) | copy-start | bytes 110596
  6.5 9.9 %copy-start.13 = (f32[45,4608]{1,0:T(8,128)S(1)}, f32[45,4608]{1,0:T(8,128)}, u32[]{:S(2)}) copy-start(f32[45,4608]{1,0:T(8,128)} %param.17) | copy-start | bytes 2488324
  10.1 12.7 %copy-start.7 = (f32[45,3072]{1,0:T(8,128)S(1)}, f32[45,3072]{1,0:T(8,128)}, u32[]{:S(2)}) copy-start(f32[45,3072]{1,0:T(8,128)} %param.16) | copy-start | bytes 1658884
  10.3 8.1 %collective-permute-start.1 = (bf16[256,45]{0,1:T(8,128)(2,1)S(1)}, bf16[256,45]{0,1:T(8,128)(2,1)S(1)}, u32[]{:S(2)}, u32[]{:S(2)}) collective-permute-start(bf16[256,45]{0,1:T(8,128)(2,1)S(1)} %get-tuple-element.26), channel_id=1, source_target_pairs={{2,0},{4,2},{6,4},{8,6},{10,8},{12,10},{14,12},{0,14},{3,1},{5,3},... | collective-permute-start | bytes 69128 | tf_op jit(solution)/shard_map/ppermute | solution.py:17
  16.3 6.5 %collective-permute-start = (bf16[256,45]{0,1:T(8,128)(2,1)S(1)}, bf16[256,45]{0,1:T(8,128)(2,1)S(1)}, u32[]{:S(2)}, u32[]{:S(2)}) collective-permute-start(bf16[256,45]{0,1:T(8,128)(2,1)S(1)} %get-tuple-element.25), channel_id=1, source_target_pairs={{0,2},{2,4},{4,6},{6,8},{8,10},{10,12},{12,14},{14,0},{1,3},{3,5},... | collective-permute-start | bytes 69128 | tf_op jit(solution)/shard_map/ppermute | solution.py:16
  25.4 31.0 %copy-start.14 = (f32[4608]{0:T(1024)S(1)}, f32[4608]{0:T(1024)}, u32[]{:S(2)}) copy-start(f32[4608]{0:T(1024)} %param.19) | copy-start | bytes 55300
  60.5 31.2 %copy-start.2 = (f32[4608,45]{1,0:T(8,128)}, f32[4608,45]{1,0:T(8,128)S(1)}, u32[]{:S(2)}) copy-start(f32[4608,45]{1,0:T(8,128)S(1)} %fusion.3) | copy-start | bytes 2488324
  91.7 4.8 %copy-start.4 = (f32[9216,45]{1,0:T(8,128)S(1)}, f32[9216,45]{1,0:T(8,128)}, u32[]{:S(2)}) copy-start(f32[9216,45]{1,0:T(8,128)} %gather_fusion.2) | copy-start | bytes 4976644
  100.8 4.7 %copy-start.6 = (f32[3072,45]{1,0:T(8,128)S(1)}, f32[3072,45]{1,0:T(8,128)}, u32[]{:S(2)}) copy-start(f32[3072,45]{1,0:T(8,128)} %get-tuple-element.13) | copy-start | bytes 1658884
  106.8 3.3 %copy-start.10 = (bf16[1,3072,45]{1,0,2:T(2,128)(2,1)S(1)}, bf16[1,3072,45]{1,0,2:T(2,128)(2,1)}, u32[]{:S(2)}) copy-start(bf16[1,3072,45]{1,0,2:T(2,128)(2,1)} %copy.178) | copy-start | bytes 829444
  106.8 3.3 %copy-start.11 = (bf16[1,3072,45]{1,0,2:T(2,128)(2,1)S(1)}, bf16[1,3072,45]{1,0,2:T(2,128)(2,1)}, u32[]{:S(2)}) copy-start(bf16[1,3072,45]{1,0,2:T(2,128)(2,1)} %copy.177) | copy-start | bytes 829444
  110.1 3.1 %copy-start.12 = (bf16[6,45,3072]{2,1,0:T(8,128)(2,1)S(1)}, bf16[6,45,3072]{2,1,0:T(8,128)(2,1)}, u32[]{:S(2)}) copy-start(bf16[6,45,3072]{2,1,0:T(8,128)(2,1)} %param.18) | copy-start | bytes 4976644
  117.0 2.3 copy-start.18
  121.8 4.0 %copy-start.20 = (s32[1,8]{1,0:T(1,128)S(1)}, s32[1,8]{1,0:T(1,128)}, u32[]{:S(2)}) copy-start(s32[1,8]{1,0:T(1,128)} %param.25) | copy-start | bytes 100
  121.8 45.8 %all-to-all-start = ((bf16[16,450,128]{2,1,0:T(8,128)(2,1)}), bf16[16,450,128]{2,1,0:T(8,128)(2,1)S(1)}, u32[]{:S(2)}, u32[]{:S(2)}) async-start(bf16[16,450,128]{2,1,0:T(8,128)(2,1)} %copy.181), calls=%async_computation | async-start | bytes 3735552 | tf_op jit(solution)/shard_map/all_to_all | solution.py:96
  125.5 89.6 %all-reduce.3.cloned.1.call-start = ((), (), s32[]{:S(2)}) async-start(), calls=%async_computation.3 | async-start | bytes 4194304 | tf_op jit(solution)/shard_map/psum | solution.py:102
  169.2 3.7 %copy-start.5 = (f32[3072,45]{0,1:T(8,128)S(1)}, f32[3072,45]{0,1:T(8,128)}, u32[]{:S(2)}) copy-start(f32[3072,45]{0,1:T(8,128)} %get-tuple-element.8) | copy-start | bytes 1658884
  172.8 4.0 %copy-start.22 = (s32[1,24]{1,0:T(1,128)S(1)}, s32[1,24]{1,0:T(1,128)}, u32[]{:S(2)}) copy-start(s32[1,24]{1,0:T(1,128)} %param.26) | copy-start | bytes 292
  172.8 4.1 %copy-start.19 = (bf16[512]{0:T(512)(128)(2,1)S(1)}, bf16[512]{0:T(512)(128)(2,1)}, u32[]{:S(2)}) copy-start(bf16[512]{0:T(512)(128)(2,1)} %param.28) | copy-start | bytes 3076
  172.8 4.1 %copy-start.24 = (bf16[256]{0:T(256)(128)(2,1)S(1)}, bf16[256]{0:T(256)(128)(2,1)}, u32[]{:S(2)}) copy-start(bf16[256]{0:T(256)(128)(2,1)} %param.30) | copy-start | bytes 1540
  172.9 83.3 %reduce-scatter.5.cloned.1.call-start = ((), (), s32[]{:S(2)}) async-start(), calls=%async_computation.4 | async-start | bytes 552960
  174.8 3.9 %collective-permute-start.3 = (bf16[256,45]{0,1:T(8,128)(2,1)S(1)}, bf16[256,45]{0,1:T(8,128)(2,1)S(1)}, u32[]{:S(2)}, u32[]{:S(2)}) collective-permute-start(bf16[256,45]{0,1:T(8,128)(2,1)S(1)} %get-tuple-element.21), channel_id=1, source_target_pairs={{2,0},{4,2},{6,4},{8,6},{10,8},{12,10},{14,12},{0,14},{3,1},{5,3},... | collective-permute-start | bytes 69128 | tf_op jit(solution)/shard_map/ppermute | solution.py:17
  174.9 6.5 %collective-permute-start.2 = (bf16[256,45]{0,1:T(8,128)(2,1)S(1)}, bf16[256,45]{0,1:T(8,128)(2,1)S(1)}, u32[]{:S(2)}, u32[]{:S(2)}) collective-permute-start(bf16[256,45]{0,1:T(8,128)(2,1)S(1)} %get-tuple-element.20), channel_id=1, source_target_pairs={{0,2},{2,4},{4,6},{6,8},{8,10},{10,12},{12,14},{14,0},{1,3},{3,5},... | collective-permute-start | bytes 69128 | tf_op jit(solution)/shard_map/ppermute | solution.py:16
  184.0 31.0 %copy-start.23 = (bf16[256,90]{0,1:T(8,128)(2,1)S(1)}, bf16[256,90]{0,1:T(8,128)(2,1)}, u32[]{:S(2)}) copy-start(bf16[256,90]{0,1:T(8,128)(2,1)} %param.31) | copy-start | bytes 138244
  215.1 3.7 %copy-start.3 = (f32[4608,45]{1,0:T(8,128)S(1)}, f32[4608,45]{1,0:T(8,128)}, u32[]{:S(2)}) copy-start(f32[4608,45]{1,0:T(8,128)} %copy-done.2) | copy-start | bytes 2488324
  223.5 32.7 %copy-start.21 = (s32[1,8]{1,0:T(1,128)S(1)}, s32[1,8]{1,0:T(1,128)}, u32[]{:S(2)}) copy-start(s32[1,8]{1,0:T(1,128)} %param.25) | copy-start | bytes 100
  258.2 13.6 %all-to-all-start.1 = ((bf16[16,45,128]{2,1,0:T(8,128)(2,1)}), bf16[16,45,128]{2,1,0:T(8,128)(2,1)S(1)}, u32[]{:S(2)}, u32[]{:S(2)}) async-start(bf16[16,45,128]{2,1,0:T(8,128)(2,1)} %copy.184), calls=%async_computation.1 | async-start | bytes 393216 | tf_op jit(solution)/shard_map/all_to_all | solution.py:120
  271.8 1.2 copy-start.9
  272.2 1.8 copy-start.1
  (1 other events, 1.1 us)
Sparse Core Ops, SparseCore 0:
  173.0 19.3 all-reduce.2
  218.9 5.0 reduce-scatter.4
where the time goes:
time: 282 us; the launch traced here: 281 us
  local copies, waits for them, and re-layouts  173 us (61%)
  waiting for transfers between devices  50.8 us (18%)
  other arithmetic  19.1 us (7%)
  starting transfers between devices  15.4 us (5%)
  between operations  13.8 us (5%)
  matrix products  8.76 us (3%)
    gather x2, local copies, waits for them, and re-layouts, substep(): jnp.take(moved, cell_edges[0].reshape(-1), axis=0, mode='clip')  63.9 us
    gather x2, local copies, waits for them, and re-layouts, substep(): jnp.take(extended, edge_cells[0].reshape(-1), axis=0, mode='clip')  62 us
    all_to_all x1, waiting for transfers between devices, body(): lax.all_to_all(outgoing, 'cells', split_axis=0, concat_axis=0, tiled=True)  41.8 us
    unnamed x59, local copies, waits for them, and re-layouts  14.8 us
    slice x2, local copies, waits for them, and re-layouts, substep(): beside_all[0]  9.07 us
    sub x2, other arithmetic, substep(): moved = velocity_rows - edge_coef[:, None] * (both[1] - both[0])  8.66 us
    ppermute x2, waiting for transfers between devices, with_halo(): before = lax.ppermute(last, axis, up)  7.2 us
    ppermute x2, starting transfers between devices, with_halo(): after = lax.ppermute(first, axis, down)  6.11 us
  transfers between devices with their start and end apart: 8, of which 4 were waited for; matrix products, arithmetic and copies ran while one was open for 30% of the time, Pallas kernels for 0%

commit v1 on v0

v1 whole, which is shorter than its diff:
```python
import functools
import jax
import jax.numpy as jnp
from jax import lax
from jax.experimental import pallas as pl
from jax.experimental.pallas import tpu as pltpu
from jax.sharding import PartitionSpec as P

BLK = 128
LANES = 128
NDER = 4
F32 = jnp.float32
BF16 = jnp.bfloat16
VMEM = pl.BlockSpec(memory_space=pltpu.VMEM)
SMEM = pl.BlockSpec(memory_space=pltpu.SMEM)
PARAMS = pltpu.CompilerParams(vmem_limit_bytes=56 * 1024 * 1024)


def up16(n):
    return -(-n // 16) * 16


def row(ref, i):
    return ref[pl.ds(i, 1), :]


def level_mask(levels, shape):
    return lax.broadcasted_iota(jnp.int32, shape, 1) < levels


def loop(count, step, body):
    def run(i, carry):
        body(pl.multiple_of(i * step, step))
        return carry

    lax.fori_loop(0, count // step, run, 0)


def pack_rows(index_ref, rows_ref, out_ref, stage):
    count = index_ref.shape[0]

    def some(base):
        for u in range(16):
            stage[pl.ds(base + u, 1), :] = row(rows_ref, index_ref[base + u])

    loop(count, 16, some)
    out_ref[...] = stage[...].astype(out_ref.dtype)


def open_kernel(halo_ref, height_ref, coef_ref, rows_ref, out_ref, wide, stage):
    levels, cells = height_ref.shape
    wide[...] = jnp.zeros_like(wide)
    wide[0:levels, :] = height_ref[...]
    wide[levels : levels + 3, :] = coef_ref[...]
    for b in range(cells // BLK):
        cols = slice(b * BLK, (b + 1) * BLK)
        rows_ref[cols, :] = wide[:, cols].T
    pack_rows(halo_ref, rows_ref, out_ref, stage)


def edges_and_cells(levels, ec_ref, ce_ref, h_ref, v_ref, before_ref, after_ref, v_out, ext, dif, beside):
    cells, edges = h_ref.shape[0], v_ref.shape[0]
    margin = before_ref.shape[0]
    ext[0:cells, :] = h_ref[...]
    ext[cells : cells + margin, :] = before_ref[...].astype(F32)
    ext[cells + margin : cells + 2 * margin, :] = after_ref[...].astype(F32)

    def some_edges(base):
        for u in range(16):
            e = base + u
            dif[pl.ds(e, 1), :] = row(ext, ec_ref[edges + e]) - row(ext, ec_ref[e])

    loop(edges, 16, some_edges)

    def move(base):
        at = pl.ds(base, 128)
        v = v_ref[at, :]
        coef = v[:, levels : levels + 1]
        v_out[at, :] = jnp.where(level_mask(levels, v.shape), v - coef * dif[at, :], v)

    loop(edges, 128, move)

    def some_cells(base):
        for u in range(8):
            c = base + u
            for k in range(3):
                beside[k, pl.ds(c, 1), :] = row(v_out, ce_ref[k * cells + c])

    loop(cells, 8, some_cells)


def spread_of(levels, h, a0, a1, a2):
    return (
        h[:, levels : levels + 1] * a0
        + h[:, levels + 1 : levels + 2] * a1
        + h[:, levels + 2 : levels + 3] * a2
    )


def first_kernel(
    levels, ec_ref, ce_ref, halo_ref, sb_ref, h_ref, v_ref, before_ref, after_ref, tr_ref,
    h_out, v_out, pack_out, own_ref, other_ref, ext, dif, beside, stage,
):
    edges_and_cells(levels, ec_ref, ce_ref, h_ref, v_ref, before_ref, after_ref, v_out, ext, dif, beside)
    cells = h_ref.shape[0]
    pad = own_ref.shape[0] // (NDER + tr_ref.shape[0])

    def move(base):
        at = pl.ds(base, 128)
        h = h_ref[at, :]
        div = spread_of(levels, h, beside[0, at, :], beside[1, at, :], beside[2, at, :])
        h_out[at, :] = jnp.where(level_mask(levels, h.shape), h - div, h)

    loop(cells, 128, move)
    pack_rows(halo_ref, h_out, pack_out, stage)
    me = lax.axis_index("stack")
    half = sb_ref.shape[0] // 2
    third = 1.0 / 3.0
    for which, x_ref in ((me, own_ref), (1 - me, other_ref)):
        for j in range(half):
            b = jnp.maximum(sb_ref[which * half + j], 0)
            at = pl.ds(pl.multiple_of(b * BLK, BLK), BLK)
            cols = slice(j * BLK, (j + 1) * BLK)
            h, a0, a1, a2 = h_ref[at, :], beside[0, at, :], beside[1, at, :], beside[2, at, :]
            fields = (
                h_out[at, :],
                spread_of(levels, h, a0, a1, a2),
                (a0 * a0 + a1 * a1 + a2 * a2) * third,
                (a0 + a1 + a2) * third,
            )
            for q, field in enumerate(fields):
                x_ref[q * pad : (q + 1) * pad, cols] = field.T[0:pad, :].astype(BF16)
            for t in range(tr_ref.shape[0]):
                q = NDER + t
                x_ref[q * pad : (q + 1) * pad, cols] = tr_ref[t, :, at]


def second_kernel(levels, ec_ref, ce_ref, h_ref, v_ref, before_ref, after_ref, out_ref, moved, ext, dif, beside):
    edges_and_cells(levels, ec_ref, ce_ref, h_ref, v_ref, before_ref, after_ref, moved, ext, dif, beside)
    for b in range(h_ref.shape[0] // BLK):
        at = slice(b * BLK, (b + 1) * BLK)
        h = h_ref[at, :]
        div = spread_of(levels, h, beside[0, at, :], beside[1, at, :], beside[2, at, :])
        out_ref[:, at] = (h - div).T[0:levels, :]


def physics_kernel(sizes, x_own, x_other, p_own, p_other, keep_ref, send_ref):
    feats, hid, half, pad = sizes
    me = lax.axis_index("stack")
    bias_one = p_own[0:hid, feats + 1 : feats + 2].astype(F32)

    def dot(a, b):
        return jnp.dot(a, b, preferred_element_type=F32)

    def silu(v):
        return (v / (1.0 + jnp.exp(-v))).astype(BF16)

    for base in range(0, x_own.shape[1], 256):
        at = slice(base, base + 256)
        one = dot(p_own[0:hid, 0:feats], x_own[:, at]) + dot(p_other[0:hid, 0:feats], x_other[:, at])
        one = silu(one + bias_one)
        twos = []
        for p in (p_own, p_other):
            bias_two = p[0:half, feats : feats + 1].astype(F32)
            twos.append(silu(dot(p[hid : hid + half, :], one) + bias_two))
        for ref, which in ((keep_ref, me), (send_ref, 1 - me)):
            start = pl.multiple_of(hid + half + which * pad, 16)
            total = dot(p_own[pl.ds(start, pad), 0:half], twos[0])
            total += dot(p_other[pl.ds(start, pad), 0:half], twos[1])
            ref[:, at] = total.astype(BF16)


def close_kernel(sb_ref, count_ref, h_ref, keep_ref, got_ref, out_ref):
    levels = h_ref.shape[0]
    me = lax.axis_index("stack")
    half = sb_ref.shape[0] // 2
    out_ref[...] = h_ref[...]
    lane = lax.broadcasted_iota(jnp.int32, (keep_ref.shape[0], BLK), 1)
    for which, ref in ((me, keep_ref), (1 - me, got_ref)):
        for j in range(half):
            s = which * half + j
            b = jnp.maximum(sb_ref[s], 0)
            at = pl.ds(pl.multiple_of(b * BLK, BLK), BLK)
            tend = ref[:, j * BLK : (j + 1) * BLK].astype(F32)
            tend = jnp.where(lane < count_ref[s], tend, 0.0)
            out_ref[:, at] = out_ref[:, at] + tend[0:levels, :]


def body(
    height, velocity, tracers, edge_coef, cell_coef, halo_send, edge_cells, cell_edges,
    send_block, recv_slot, block_count, w_first, b_first, w_second, b_second, w_third,
):
    levels, cells = height.shape
    edges = velocity.shape[1]
    margin = halo_send.shape[1] // 2
    slots = send_block.shape[1]
    half_slots = slots // 2
    cap = slots // lax.axis_size("cells")
    nq = NDER + tracers.shape[0]
    pad = up16(levels + 3)
    feats = nq * pad
    hid, half = w_second.shape
    ring = ("cells", "role")
    size = lax.axis_size(ring)
    up = [(i, (i + 1) % size) for i in range(size)]
    down = [(j, i) for i, j in up]
    swap = [(0, 1), (1, 0)]
    halo = halo_send.reshape(-1)
    ec = edge_cells.reshape(-1)
    ce = cell_edges.reshape(-1)
    sb = send_block.reshape(-1)

    def shape(dims, dtype):
        return jax.ShapeDtypeStruct(dims, dtype)

    def exchange(packed):
        before = lax.ppermute(packed[margin:], ring, up)
        after = lax.ppermute(packed[:margin], ring, down)
        return before, after

    h_rows, packed = pl.pallas_call(
        open_kernel,
        out_shape=(shape((cells, LANES), F32), shape((2 * margin, LANES), BF16)),
        in_specs=[SMEM, VMEM, VMEM],
        out_specs=(VMEM, VMEM),
        scratch_shapes=[pltpu.VMEM((LANES, cells), F32), pltpu.VMEM((2 * margin, LANES), F32)],
        compiler_params=PARAMS,
        name="open_rows",
    )(halo, height, cell_coef)
    before, after = exchange(packed)

    one = w_first.reshape(levels, nq, hid).transpose(2, 1, 0)
    one = jnp.pad(one, ((0, 0), (0, 0), (0, pad - levels))).reshape(hid, feats)
    bias_two = jnp.pad(b_second, (0, hid - half))
    one = jnp.concatenate([one, bias_two[:, None], b_first[:, None]], axis=1)
    one = jnp.pad(one, ((0, 0), (0, hid - one.shape[1])))
    three = jnp.pad(w_third.T.reshape(2, levels, half), ((0, 0), (0, pad - levels), (0, 0)))
    three = jnp.pad(three.reshape(2 * pad, half), ((0, 0), (0, hid - half)))
    mine = jnp.concatenate([one, w_second.T, three], axis=0)
    theirs = lax.ppermute(mine, "stack", swap)

    v_rows = jnp.pad(
        jnp.concatenate([velocity, edge_coef[None]], axis=0), ((0, LANES - levels - 1), (0, 0))
    ).T
    tracers = jnp.pad(tracers, ((0, 0), (0, pad - levels), (0, 0)))

    wanted = lax.all_gather(recv_slot[0], "cells")
    slot = jnp.arange(slots, dtype=jnp.int32)
    entry = lax.axis_index("cells") * cap + slot % cap
    dest = jnp.arange(wanted.shape[0], dtype=jnp.int32)
    match = (wanted[None] == entry[:, None, None]) & (dest[None, :, None] == (slot // cap)[:, None, None])
    block = jnp.arange(cells // BLK, dtype=jnp.int32)
    counts = jnp.sum(jnp.where(sb[:, None] == block[None], block_count[0][None], 0), axis=1)
    counts = jnp.where(jnp.any(match, axis=(1, 2)), counts, 0).astype(jnp.int32)

    field_scratch = [
        pltpu.VMEM((cells + 2 * margin, LANES), F32),
        pltpu.VMEM((edges, LANES), F32),
        pltpu.VMEM((3, cells, LANES), F32),
    ]
    x_shape = shape((feats, half_slots * BLK), BF16)
    h_rows, v_rows, packed, x_own, x_send = pl.pallas_call(
        functools.partial(first_kernel, levels),
        out_shape=(
            shape((cells, LANES), F32),
            shape((edges, LANES), F32),
            shape((2 * margin, LANES), BF16),
            x_shape,
            x_shape,
        ),
        in_specs=[SMEM] * 4 + [VMEM] * 5,
        out_specs=(VMEM,) * 5,
        scratch_shapes=field_scratch + [pltpu.VMEM((2 * margin, LANES), F32)],
        compiler_params=PARAMS,
        name="first_substep",
    )(ec, ce, halo, sb, h_rows, v_rows, before, after, tracers)
    x_other = lax.ppermute(x_send, "stack", swap)
    before, after = exchange(packed)

    t_shape = shape((pad, half_slots * BLK), BF16)
    keep, send = pl.pallas_call(
        functools.partial(physics_kernel, (feats, hid, half, pad)),
        out_shape=(t_shape, t_shape),
        in_specs=[VMEM] * 4,
        out_specs=(VMEM, VMEM),
        compiler_params=PARAMS,
        cost_estimate=pl.CostEstimate(flops=2 * 10**9, bytes_accessed=4 * 10**6, transcendentals=10**6),
        name="physics",
    )(x_own, x_other, mine, theirs)
    got = lax.ppermute(send, "stack", swap)

    h_second = pl.pallas_call(
        functools.partial(second_kernel, levels),
        out_shape=shape((levels, cells), F32),
        in_specs=[SMEM] * 2 + [VMEM] * 4,
        out_specs=VMEM,
        scratch_shapes=[pltpu.VMEM((edges, LANES), F32)] + field_scratch,
        compiler_params=PARAMS,
        cost_estimate=pl.CostEstimate(flops=2 * 10**10, bytes_accessed=50 * 10**6, transcendentals=0),
        name="second_substep",
    )(ec, ce, h_rows, v_rows, before, after)

    return pl.pallas_call(
        close_kernel,
        out_shape=shape((levels, cells), F32),
        in_specs=[SMEM] * 2 + [VMEM] * 3,
        out_specs=VMEM,
        compiler_params=PARAMS,
        name="close_add",
    )(sb, counts, h_second, keep, got)


def solution(mesh):
    placed = (
        P("stack", ("groups", "cells", "role")),
        P("stack", ("groups", "cells", "role")),
        P(None, "stack", ("groups", "cells", "role")),
        P(("cells", "role")),
        P(None, ("cells", "role")),
        P(("cells", "role"), None),
        P(("cells", "role"), None, None),
        P(("cells", "role"), None, None),
        P(("cells", "role"), None),
        P(("cells", "role"), None),
        P(("cells", "role"), None),
        P("stack", None),
        P(),
        P(None, "stack"),
        P("stack"),
        P("stack", None),
    )
    return jax.shard_map(
        body,
        mesh=mesh,
        in_specs=placed,
        out_specs=P("stack", ("groups", "cells", "role")),
        check_vma=False,
    )
```

time: 282 us -> 106 us (0.38)
  local copies, waits for them, and re-layouts: 173 us -> 12.3 us
  Pallas kernels: 0 us -> 70.2 us
  waiting for transfers between devices: 50.8 us -> 0.02 us
  other arithmetic: 19.1 us -> 2.06 us
  between operations: 13.8 us -> 0.27 us
  blocking collectives: 0 us -> 9.42 us
  matrix products: 8.76 us -> 0 us
  starting transfers between devices: 15.4 us -> 10.9 us
    gather x9 -> x0, local copies, waits for them, and re-layouts: 130 us -> none  [the longest x2 63.9 us: substep(): jnp.take(moved, cell_edges[0].reshape(-1), axis=0, mode='clip')]
    pallas_call x0 -> x5, Pallas kernels: none -> 70.2 us  [the longest x1 31.6 us: body(): pl.pallas_call(functools.partial(first_kernel, levels), out_shape=(shape(...]
    all_to_all x2 -> x0, waiting for transfers between devices: 41.8 us -> none  [the longest x1 41.8 us: body(): lax.all_to_all(outgoing, 'cells', split_axis=0, concat_axis=0, tiled=True)]
    unnamed x59 -> x36, local copies, waits for them, and re-layouts: 14.8 us -> 4.21 us
    all_gather x0 -> x1, blocking collectives: none -> 9.42 us  [body(): wanted = lax.all_gather(recv_slot[0], 'cells')]
    ppermute x4 -> x7, waiting for transfers between devices: 8.91 us -> 0.02 us  [the longest x2 0.01 us: exchange(): after = lax.ppermute(packed[:margin], ring, down)]
    dot_general x5 -> x0, matrix products: 8.76 us -> none  [the longest x1 3.62 us: body(): jnp.einsum('nfi,fh->nhi', picked, w_first, preferred_element_type=jnp.flo...]
    sub x2 -> x0, other arithmetic: 8.66 us -> none  [substep(): moved = velocity_rows - edge_coef[:, None] * (both[1] - both[0])]
  transfers between devices with their start and end apart: 8 -> 7, of which waited for: 4 -> 0; matrix products, arithmetic and copies ran while one was open for 30% -> 9% of each run, Pallas kernels for 0% -> 62%
where the time goes in v1:
time: 106 us; the launch traced here: 105 us
  Pallas kernels  70.2 us (66%)
  local copies, waits for them, and re-layouts  12.3 us (12%)
  starting transfers between devices  10.9 us (10%)
  blocking collectives  9.42 us (9%)
  other arithmetic  2.06 us (2%)
    pallas_call x1, Pallas kernels, body(): pl.pallas_call(functools.partial(first_kernel, levels), out_shape=(shape(...  31.6 us
    pallas_call x1, Pallas kernels, body(): pl.pallas_call(functools.partial(second_kernel, levels), out_shape=shape(...  25.8 us
    all_gather x1, blocking collectives, body(): wanted = lax.all_gather(recv_slot[0], 'cells')  9.42 us
    pallas_call x1, Pallas kernels, body(): pl.pallas_call(functools.partial(physics_kernel, (feats, hid, half, pad))...  7.4 us
    ppermute x2, starting transfers between devices, exchange(): after = lax.ppermute(packed[:margin], ring, down)  7.23 us
    unnamed x36, local copies, waits for them, and re-layouts  4.21 us
    ppermute x2, starting transfers between devices, exchange(): before = lax.ppermute(packed[margin:], ring, up)  3.64 us
    pallas_call x1, Pallas kernels, body(): pl.pallas_call(open_kernel, out_shape=(shape((cells, LANES), F32), shape(...  3.33 us
  transfers between devices with their start and end apart: 7, of which 0 were waited for; matrix products, arithmetic and copies ran while one was open for 9% of the time, Pallas kernels for 62%

profile of v1, /device:TPU:0, one launch (start us, length us, event | category | flops | bytes accessed | tf_op | source)
XLA Modules:
  0.0 105.1 jit_solution(1424249910388452996)
XLA Ops:
  0.0 3.3 %open_rows.1 = (f32[3072,128]{1,0:T(8,128)}, bf16[512,128]{1,0:T(8,128)(2,1)}) custom-call(s32[512]{0:T(512)} %bitcast.20, f32[45,3072]{1,0:T(8,128)} %height_ref.1, f32[3,3072]{1,0:T(4,128)} %coef_ref.1), custom_call_target="tpu_custom_call" | custom-call | tf_op jit(solution)/shard_map/open_rows/pallas_call | solution.py:221
  3.3 0.9 fusion.9
  4.2 3.0 %collective-permute-start = (bf16[256,128]{1,0:T(8,128)(2,1)S(1)}, bf16[256,128]{1,0:T(8,128)(2,1)S(1)}, u32[]{:S(2)}, u32[]{:S(2)}) collective-permute-start(bf16[256,128]{1,0:T(8,128)(2,1)S(1)} %get-tuple-element.26), channel_id=1, source_target_pairs={{0,2},{2,4},{4,6},{6,8},{8,10},{10,12},{12,14},{14,0},{1,3},{3,5},... | collective-permute-start | bytes 196616 | tf_op jit(solution)/shard_map/ppermute | solution.py:217
  7.2 3.1 %collective-permute-start.1 = (bf16[256,128]{1,0:T(8,128)(2,1)S(1)}, bf16[256,128]{1,0:T(8,128)(2,1)S(1)}, u32[]{:S(2)}, u32[]{:S(2)}) collective-permute-start(bf16[256,128]{1,0:T(8,128)(2,1)S(1)} %get-tuple-element.25), channel_id=1, source_target_pairs={{2,0},{4,2},{6,4},{8,6},{10,8},{12,10},{14,12},{0,14},{3,1},{5,3},... | collective-permute-start | bytes 196616 | tf_op jit(solution)/shard_map/ppermute | solution.py:218
  10.3 1.2 %reshape.77 = bf16[45,10,512]{2,1,0:T(8,128)(2,1)S(1)} reshape(bf16[450,512]{1,0:T(8,128)(2,1)} %param.27) | data formatting | bytes 921600 | tf_op jit(solution)/shard_map/reshape | solution.py:232
  11.6 0.3 copy.39
  11.9 0.2 copy.35
  12.2 0.1 broadcast_in_dim.36
  12.3 0.1 broadcast_in_dim.37
  12.5 0.1 copy.38
  12.7 0.2 fusion.6
  12.9 1.0 fusion.4.p_own
  13.9 0.6 reshape.74.ec_ref
  14.7 0.9 copy.33
  15.6 1.6 %pad_bitcast_fusion.v_ref = f32[4608,128]{1,0:T(8,128)} fusion(f32[46,4608]{0,1:T(8,128)S(1)} %copy.33), kind=kLoop, calls=%fused_computation | loop fusion | bytes 3207168 | tf_op jit(solution)/shard_map/transpose | solution.py:244
  17.1 0.7 copy-done
  17.9 1.4 %pad.29.tr_ref = bf16[6,48,3072]{2,1,0:T(8,128)(2,1)} pad(bf16[6,45,3072]{2,1,0:T(8,128)(2,1)S(1)} %copy-done, bf16[]{:T(256)} %constant.42.clone.1), padding=0_0x0_3x0_0 | pad | bytes 3428354 | tf_op jit(solution)/shard_map/jit(_pad)/pad | solution.py:245
  19.3 9.4 %all-gather = s32[4,1,8]{2,1,0:T(1,128)S(1)} all-gather(s32[1,1,8]{2,1,0:T(1,128)S(1)} %bitcast.26), channel_id=1, replica_groups=mesh['groups'=2,'cells'=4,'role'=2,'stack'=2] {'cells'}, dimensions={0}, use_global_device_ids=true | all-gather | bytes 160 | tf_op jit(solution)/shard_map/all_gather | solution.py:247
  28.7 0.2 select_reduce_fusion
  29.0 0.6 copy-done.4
  29.6 31.6 %first_substep.1 = (f32[3072,128]{1,0:T(8,128)}, f32[4608,128]{1,0:T(8,128)}, bf16[512,128]{1,0:T(8,128)(2,1)}, bf16[480,1024]{1,0:T(8,128)(2,1)}, bf16[480,1024]{1,0:T(8,128)(2,1)}) custom-call(s32[9216]{0:T(1024)} %reshape.74.ec_ref, s32[9216]{0:T(1024)} %bitcast.18, s32[512]{0:T(512)} %bitcast.21, s32[16]{0:T(128)} %bitcast.23, ...), custom_call_target="tpu_custom_call" | custom-call | tf_op jit(solution)/shard_map/first_substep/pallas_call | solution.py:262
  61.2 0.1 and_reduce_fusion
  61.3 0.5 broadcast_select_fusion.count_ref
  61.8 0.9 fusion.8
  62.7 0.6 collective-permute-start.2
  63.4 4.1 %collective-permute-start.3 = (bf16[256,128]{1,0:T(8,128)(2,1)S(1)}, bf16[256,128]{1,0:T(8,128)(2,1)S(1)}, u32[]{:S(2)}, u32[]{:S(2)}) collective-permute-start(bf16[256,128]{1,0:T(8,128)(2,1)S(1)} %get-tuple-element.23), channel_id=1, source_target_pairs={{2,0},{4,2},{6,4},{8,6},{10,8},{12,10},{14,12},{0,14},{3,1},{5,3},... | collective-permute-start | bytes 196616 | tf_op jit(solution)/shard_map/ppermute | solution.py:218
  67.5 1.0 copy-done.13
  68.5 7.4 %physics.1 = (bf16[48,1024]{1,0:T(8,128)(2,1)}, bf16[48,1024]{1,0:T(8,128)(2,1)}) custom-call(bf16[480,1024]{1,0:T(8,128)(2,1)} %get-tuple-element.19.x_own, bf16[480,1024]{1,0:T(8,128)(2,1)} %copy-done.13, bf16[864,512]{1,0:T(8,128)(2,1)} %fusion.4.p_own, bf16[864,512]{1,0:T(8,128)(2,1)} %collective-permute-done.5.p_other), custom_call_target="tpu_custom_call" | custom-call | flops 2000000000 | bytes 4000000 | tf_op jit(solution)/shard_map/physics/pallas_call | solution.py:281
  76.0 0.6 copy-done.14
  76.6 25.8 %second_substep.1.h_ref = f32[45,3072]{1,0:T(8,128)} custom-call(s32[9216]{0:T(1024)} %reshape.74.ec_ref, s32[9216]{0:T(1024)} %bitcast.19, f32[3072,128]{1,0:T(8,128)} %get-tuple-element.16.h_ref, f32[4608,128]{1,0:T(8,128)} %get-tuple-element.17.v_ref, bf16[256,128]{1,0:T(8,128)(2,1)} %copy-done.14, bf16[256,128]{1,0:T(8,128)(2,1)} %copy-done.15), custom_call_target="tpu_custom_call" | custom-call | flops 20000000000 | bytes 50000000 | tf_op jit(solution)/shard_map/second_substep/pallas_call | solution.py:292
  102.4 0.6 copy-done.3
  103.0 2.1 %close_add.1 = f32[45,3072]{1,0:T(8,128)} custom-call(s32[16]{0:T(128)} %bitcast.24, s32[16]{0:T(128)} %broadcast_select_fusion.count_ref, f32[45,3072]{1,0:T(8,128)} %second_substep.1.h_ref, bf16[48,1024]{1,0:T(8,128)(2,1)} %get-tuple-element.21.keep_ref, bf16[48,1024]{1,0:T(8,128)(2,1)} %copy-done.3), custom_call_target="tpu_custom_call" | custom-call | tf_op jit(solution)/shard_map/close_add/pallas_call | solution.py:303
  (48 shorter events, 0.4 us)
Async XLA Ops:
  4.2 24.7 %collective-permute-start = (bf16[256,128]{1,0:T(8,128)(2,1)S(1)}, bf16[256,128]{1,0:T(8,128)(2,1)S(1)}, u32[]{:S(2)}, u32[]{:S(2)}) collective-permute-start(bf16[256,128]{1,0:T(8,128)(2,1)S(1)} %get-tuple-element.26), channel_id=1, source_target_pairs={{0,2},{2,4},{4,6},{6,8},{8,10},{10,12},{12,14},{14,0},{1,3},{3,5},... | collective-permute-start | bytes 196616 | tf_op jit(solution)/shard_map/ppermute | solution.py:217
  7.2 21.7 %collective-permute-start.1 = (bf16[256,128]{1,0:T(8,128)(2,1)S(1)}, bf16[256,128]{1,0:T(8,128)(2,1)S(1)}, u32[]{:S(2)}, u32[]{:S(2)}) collective-permute-start(bf16[256,128]{1,0:T(8,128)(2,1)S(1)} %get-tuple-element.25), channel_id=1, source_target_pairs={{2,0},{4,2},{6,4},{8,6},{10,8},{12,10},{14,12},{0,14},{3,1},{5,3},... | collective-permute-start | bytes 196616 | tf_op jit(solution)/shard_map/ppermute | solution.py:218
  11.5 0.7 copy-start.12
  11.5 0.8 copy-start.10
  11.5 1.0 copy-start.2
  11.6 1.1 %copy-start.6 = (bf16[256,90]{0,1:T(8,128)(2,1)S(1)}, bf16[256,90]{0,1:T(8,128)(2,1)}, u32[]{:S(2)}) copy-start(bf16[256,90]{0,1:T(8,128)(2,1)} %param.31) | copy-start | bytes 138244
  12.5 1.4 %copy-start.7 = (s32[1,2,4608]{2,1,0:T(2,128)S(1)}, s32[1,2,4608]{2,1,0:T(2,128)}, u32[]{:S(2)}) copy-start(s32[1,2,4608]{2,1,0:T(2,128)} %param.22) | copy-start | bytes 110596
  12.7 1.9 %copy-start.8 = (f32[4608]{0:T(1024)S(1)}, f32[4608]{0:T(1024)}, u32[]{:S(2)}) copy-start(f32[4608]{0:T(1024)} %param.19) | copy-start | bytes 55300
  12.7 1.9 %copy-start.1 = (f32[45,4608]{1,0:T(8,128)S(1)}, f32[45,4608]{1,0:T(8,128)}, u32[]{:S(2)}) copy-start(f32[45,4608]{1,0:T(8,128)} %param.17) | copy-start | bytes 2488324
  13.9 53.6 %collective-permute-start.5 = (bf16[864,512]{1,0:T(8,128)(2,1)}, bf16[864,512]{1,0:T(8,128)(2,1)}, u32[]{:S(2)}, u32[]{:S(2)}) collective-permute-start(bf16[864,512]{1,0:T(8,128)(2,1)} %fusion.4.p_own), channel_id=1, source_target_pairs={{0,1},{1,0},{2,3},{3,2},{4,5},{5,4},{6,7},{7,6},{8,9},{9,8},{10,11... | collective-permute-start | bytes 2654216 | tf_op jit(solution)/shard_map/ppermute | solution.py:240
  15.5 2.3 %copy-start = (bf16[6,45,3072]{2,1,0:T(8,128)(2,1)S(1)}, bf16[6,45,3072]{2,1,0:T(8,128)(2,1)}, u32[]{:S(2)}) copy-start(bf16[6,45,3072]{2,1,0:T(8,128)(2,1)} %param.18) | copy-start | bytes 4976644
  17.9 1.4 %copy-start.11 = (s32[1,8]{1,0:T(1,128)S(1)}, s32[1,8]{1,0:T(1,128)}, u32[]{:S(2)}) copy-start(s32[1,8]{1,0:T(1,128)} %param.25) | copy-start | bytes 100
  17.9 10.9 %copy-start.9 = (s32[1,16]{1,0:T(1,128)S(1)}, s32[1,16]{1,0:T(1,128)}, u32[]{:S(2)}) copy-start(s32[1,16]{1,0:T(1,128)} %param.24) | copy-start | bytes 196
  17.9 10.9 %copy-start.16 = (s32[1,24]{1,0:T(1,128)S(1)}, s32[1,24]{1,0:T(1,128)}, u32[]{:S(2)}) copy-start(s32[1,24]{1,0:T(1,128)} %param.26) | copy-start | bytes 292
  28.9 0.6 copy-start.4
  28.9 0.6 copy-start.5
  61.2 6.3 %collective-permute-start.4 = (bf16[480,1024]{1,0:T(8,128)(2,1)}, bf16[480,1024]{1,0:T(8,128)(2,1)S(1)}, u32[]{:S(2)}, u32[]{:S(2)}) collective-permute-start(bf16[480,1024]{1,0:T(8,128)(2,1)} %get-tuple-element.20), channel_id=1, source_target_pairs={{0,1},{1,0},{2,3},{3,2},{4,5},{5,4},{6,7},{7,6},{8,9},{9,8},{10,11... | collective-permute-start | bytes 2949128 | tf_op jit(solution)/shard_map/ppermute | solution.py:277
  62.7 13.2 %collective-permute-start.2 = (bf16[256,128]{1,0:T(8,128)(2,1)S(1)}, bf16[256,128]{1,0:T(8,128)(2,1)S(1)}, u32[]{:S(2)}, u32[]{:S(2)}) collective-permute-start(bf16[256,128]{1,0:T(8,128)(2,1)S(1)} %get-tuple-element.24), channel_id=1, source_target_pairs={{0,2},{2,4},{4,6},{6,8},{8,10},{10,12},{12,14},{14,0},{1,3},{3,5},... | collective-permute-start | bytes 196616 | tf_op jit(solution)/shard_map/ppermute | solution.py:217
  63.4 12.6 %collective-permute-start.3 = (bf16[256,128]{1,0:T(8,128)(2,1)S(1)}, bf16[256,128]{1,0:T(8,128)(2,1)S(1)}, u32[]{:S(2)}, u32[]{:S(2)}) collective-permute-start(bf16[256,128]{1,0:T(8,128)(2,1)S(1)} %get-tuple-element.23), channel_id=1, source_target_pairs={{2,0},{4,2},{6,4},{8,6},{10,8},{12,10},{14,12},{0,14},{3,1},{5,3},... | collective-permute-start | bytes 196616 | tf_op jit(solution)/shard_map/ppermute | solution.py:218
  67.5 1.0 copy-start.13
  75.9 26.4 %collective-permute-start.6 = (bf16[48,1024]{1,0:T(8,128)(2,1)}, bf16[48,1024]{1,0:T(8,128)(2,1)S(1)}, u32[]{:S(2)}, u32[]{:S(2)}) collective-permute-start(bf16[48,1024]{1,0:T(8,128)(2,1)} %get-tuple-element.22), channel_id=1, source_target_pairs={{0,1},{1,0},{2,3},{3,2},{4,5},{5,4},{6,7},{7,6},{8,9},{9,8},{10,11... | collective-permute-start | bytes 294920 | tf_op jit(solution)/shard_map/ppermute | solution.py:290
  75.9 0.6 copy-start.14
  76.0 0.6 copy-start.15
  102.4 0.6 copy-start.3

commit v2 on v1

--- a/solution.py
+++ b/solution.py
@@ -16,6 +16,12 @@
 PARAMS = pltpu.CompilerParams(vmem_limit_bytes=56 * 1024 * 1024)
 
 
+def remote_params(collective_id):
+    return pltpu.CompilerParams(
+        vmem_limit_bytes=56 * 1024 * 1024, collective_id=collective_id, has_side_effects=True
+    )
+
+
 def up16(n):
     return -(-n // 16) * 16
 
@@ -47,15 +53,76 @@
     out_ref[...] = stage[...].astype(out_ref.dtype)
 
 
-def open_kernel(halo_ref, height_ref, coef_ref, rows_ref, out_ref, wide, stage):
-    levels, cells = height_ref.shape
-    wide[...] = jnp.zeros_like(wide)
-    wide[0:levels, :] = height_ref[...]
-    wide[levels : levels + 3, :] = coef_ref[...]
-    for b in range(cells // BLK):
+def remote(src, dst, sems, at, target):
+    return pltpu.make_async_remote_copy(
+        src_ref=src,
+        dst_ref=dst,
+        send_sem=sems.at[0, at],
+        recv_sem=sems.at[1, at],
+        device_id=target,
+        device_id_type=pl.DeviceIdType.MESH,
+    )
+
+
+def greet(targets):
+    barrier = pltpu.get_barrier_semaphore()
+    for target in targets:
+        pl.semaphore_signal(barrier, inc=1, device_id=target, device_id_type=pl.DeviceIdType.MESH)
+    pl.semaphore_wait(barrier, len(targets))
+
+
+def around_ring(n_cells, n_role):
+    size = n_cells * n_role
+    me = lax.axis_index("cells") * n_role + lax.axis_index("role")
+    found = []
+    for step in (1, size - 1):
+        there = lax.rem(me + step, size)
+        found.append({"cells": lax.div(there, n_role), "role": lax.rem(there, n_role)})
+    return found
+
+
+def halo_copies(packed, before, after, sems, ring):
+    margin = packed.shape[0] // 2
+    return [
+        remote(packed.at[pl.ds(margin, margin)], before, sems, 0, ring[0]),
+        remote(packed.at[pl.ds(0, margin)], after, sems, 1, ring[1]),
+    ]
+
+
+def to_rows(field_ref, extra_ref, rows_ref, wide):
+    levels, count = field_ref.shape
+    extra = extra_ref.shape[0]
+    wide[0:levels, 0:count] = field_ref[...]
+    wide[levels : levels + extra, 0:count] = extra_ref[...]
+    for b in range(count // BLK):
         cols = slice(b * BLK, (b + 1) * BLK)
         rows_ref[cols, :] = wide[:, cols].T
-    pack_rows(halo_ref, rows_ref, out_ref, stage)
+
+
+def open_kernel(
+    mesh_size, halo_ref, height_ref, coef_ref, velocity_ref, edge_ref, recv_ref,
+    rows_ref, v_ref, before_ref, after_ref, table_ref, wide, stage, packed, sems,
+):
+    n_cells, n_role = mesh_size
+    ring = around_ring(n_cells, n_role)
+    me = lax.axis_index("cells")
+    peers = [{"cells": lax.rem(me + step, n_cells)} for step in range(1, n_cells)]
+    greet(ring + peers)
+    copies = [
+        remote(recv_ref, table_ref.at[me], sems, 2 + i, peer) for i, peer in enumerate(peers)
+    ]
+    for copy in copies:
+        copy.start()
+    table_ref[me] = recv_ref[...]
+    wide[...] = jnp.zeros_like(wide)
+    to_rows(height_ref, coef_ref, rows_ref, wide)
+    pack_rows(halo_ref, rows_ref, packed, stage)
+    halos = halo_copies(packed, before_ref, after_ref, sems, ring)
+    for copy in halos:
+        copy.start()
+    to_rows(velocity_ref, edge_ref, v_ref, wide)
+    for copy in copies + halos:
+        copy.wait()
 
 
 def edges_and_cells(levels, ec_ref, ce_ref, h_ref, v_ref, before_ref, after_ref, v_out, ext, dif, beside):
@@ -66,11 +133,14 @@
     ext[cells + margin : cells + 2 * margin, :] = after_ref[...].astype(F32)
 
     def some_edges(base):
-        for u in range(16):
+        found = []
+        for u in range(32):
             e = base + u
-            dif[pl.ds(e, 1), :] = row(ext, ec_ref[edges + e]) - row(ext, ec_ref[e])
-
-    loop(edges, 16, some_edges)
+            found.append(row(ext, ec_ref[edges + e]) - row(ext, ec_ref[e]))
+        for u in range(32):
+            dif[pl.ds(base + u, 1), :] = found[u]
+
+    loop(edges, 32, some_edges)
 
     def move(base):
         at = pl.ds(base, 128)
@@ -81,12 +151,14 @@
     loop(edges, 128, move)
 
     def some_cells(base):
-        for u in range(8):
-            c = base + u
+        found = []
+        for u in range(16):
             for k in range(3):
-                beside[k, pl.ds(c, 1), :] = row(v_out, ce_ref[k * cells + c])
-
-    loop(cells, 8, some_cells)
+                found.append((u, k, row(v_out, ce_ref[k * cells + base + u])))
+        for u, k, value in found:
+            beside[k, pl.ds(base + u, 1), :] = value
+
+    loop(cells, 16, some_cells)
 
 
 def spread_of(levels, h, a0, a1, a2):
@@ -116,6 +188,10 @@
     me = lax.axis_index("stack")
     half = sb_ref.shape[0] // 2
     third = 1.0 / 3.0
+    for x_ref in (own_ref, other_ref):
+        for t in range(tr_ref.shape[0]):
+            end = (NDER + t + 1) * pad
+            x_ref[end - 16 : end, :] = jnp.zeros((16, x_ref.shape[1]), BF16)
     for which, x_ref in ((me, own_ref), (1 - me, other_ref)):
         for j in range(half):
             b = jnp.maximum(sb_ref[which * half + j], 0)
@@ -132,7 +208,7 @@
                 x_ref[q * pad : (q + 1) * pad, cols] = field.T[0:pad, :].astype(BF16)
             for t in range(tr_ref.shape[0]):
                 q = NDER + t
-                x_ref[q * pad : (q + 1) * pad, cols] = tr_ref[t, :, at]
+                x_ref[q * pad : q * pad + levels, cols] = tr_ref[t, :, at]
 
 
 def second_kernel(levels, ec_ref, ce_ref, h_ref, v_ref, before_ref, after_ref, out_ref, moved, ext, dif, beside):
@@ -144,9 +220,20 @@
         out_ref[:, at] = (h - div).T[0:levels, :]
 
 
-def physics_kernel(sizes, x_own, x_other, p_own, p_other, keep_ref, send_ref):
-    feats, hid, half, pad = sizes
+def physics_kernel(
+    sizes, x_own, x_mine, packed, p_own, p_other,
+    keep_ref, send_ref, before_ref, after_ref, x_other, sems,
+):
+    feats, hid, half, pad, n_cells, n_role = sizes
     me = lax.axis_index("stack")
+    ring = around_ring(n_cells, n_role)
+    twin = {"stack": 1 - me}
+    greet(ring + [twin])
+    halos = halo_copies(packed, before_ref, after_ref, sems, ring)
+    swap = remote(x_mine, x_other, sems, 2, twin)
+    for copy in [swap] + halos:
+        copy.start()
+    swap.wait()
     bias_one = p_own[0:hid, feats + 1 : feats + 2].astype(F32)
 
     def dot(a, b):
@@ -168,6 +255,8 @@
             total = dot(p_own[pl.ds(start, pad), 0:half], twos[0])
             total += dot(p_other[pl.ds(start, pad), 0:half], twos[1])
             ref[:, at] = total.astype(BF16)
+    for copy in halos:
+        copy.wait()
 
 
 def close_kernel(sb_ref, count_ref, h_ref, keep_ref, got_ref, out_ref):
@@ -190,20 +279,17 @@
     height, velocity, tracers, edge_coef, cell_coef, halo_send, edge_cells, cell_edges,
     send_block, recv_slot, block_count, w_first, b_first, w_second, b_second, w_third,
 ):
+    n_cells, n_role = lax.axis_size("cells"), lax.axis_size("role")
     levels, cells = height.shape
     edges = velocity.shape[1]
     margin = halo_send.shape[1] // 2
     slots = send_block.shape[1]
     half_slots = slots // 2
-    cap = slots // lax.axis_size("cells")
+    cap = slots // n_cells
     nq = NDER + tracers.shape[0]
     pad = up16(levels + 3)
     feats = nq * pad
     hid, half = w_second.shape
-    ring = ("cells", "role")
-    size = lax.axis_size(ring)
-    up = [(i, (i + 1) % size) for i in range(size)]
-    down = [(j, i) for i, j in up]
     swap = [(0, 1), (1, 0)]
     halo = halo_send.reshape(-1)
     ec = edge_cells.reshape(-1)
@@ -213,21 +299,29 @@
     def shape(dims, dtype):
         return jax.ShapeDtypeStruct(dims, dtype)
 
-    def exchange(packed):
-        before = lax.ppermute(packed[margin:], ring, up)
-        after = lax.ppermute(packed[:margin], ring, down)
-        return before, after
-
-    h_rows, packed = pl.pallas_call(
-        open_kernel,
-        out_shape=(shape((cells, LANES), F32), shape((2 * margin, LANES), BF16)),
-        in_specs=[SMEM, VMEM, VMEM],
-        out_specs=(VMEM, VMEM),
-        scratch_shapes=[pltpu.VMEM((LANES, cells), F32), pltpu.VMEM((2 * margin, LANES), F32)],
-        compiler_params=PARAMS,
+    halo_shape = shape((margin, LANES), BF16)
+    recv = jnp.pad(recv_slot, ((0, 0), (0, LANES - recv_slot.shape[1])), constant_values=-1)
+    h_rows, v_rows, before, after, wanted = pl.pallas_call(
+        functools.partial(open_kernel, (n_cells, n_role)),
+        out_shape=(
+            shape((cells, LANES), F32),
+            shape((edges, LANES), F32),
+            halo_shape,
+            halo_shape,
+            shape((n_cells, 1, LANES), jnp.int32),
+        ),
+        in_specs=[SMEM] + [VMEM] * 5,
+        out_specs=(VMEM,) * 5,
+        scratch_shapes=[
+            pltpu.VMEM((LANES, max(cells, edges)), F32),
+            pltpu.VMEM((2 * margin, LANES), F32),
+            pltpu.VMEM((2 * margin, LANES), BF16),
+            pltpu.SemaphoreType.DMA((2, n_cells + 1)),
+        ],
+        compiler_params=remote_params(0),
         name="open_rows",
-    )(halo, height, cell_coef)
-    before, after = exchange(packed)
+    )(halo, height, cell_coef, velocity, edge_coef[None], recv)
+    wanted = wanted.reshape(n_cells, LANES)
 
     one = w_first.reshape(levels, nq, hid).transpose(2, 1, 0)
     one = jnp.pad(one, ((0, 0), (0, 0), (0, pad - levels))).reshape(hid, feats)
@@ -239,12 +333,6 @@
     mine = jnp.concatenate([one, w_second.T, three], axis=0)
     theirs = lax.ppermute(mine, "stack", swap)
 
-    v_rows = jnp.pad(
-        jnp.concatenate([velocity, edge_coef[None]], axis=0), ((0, LANES - levels - 1), (0, 0))
-    ).T
-    tracers = jnp.pad(tracers, ((0, 0), (0, pad - levels), (0, 0)))
-
-    wanted = lax.all_gather(recv_slot[0], "cells")
     slot = jnp.arange(slots, dtype=jnp.int32)
     entry = lax.axis_index("cells") * cap + slot % cap
     dest = jnp.arange(wanted.shape[0], dtype=jnp.int32)
@@ -274,19 +362,18 @@
         compiler_params=PARAMS,
         name="first_substep",
     )(ec, ce, halo, sb, h_rows, v_rows, before, after, tracers)
-    x_other = lax.ppermute(x_send, "stack", swap)
-    before, after = exchange(packed)
 
     t_shape = shape((pad, half_slots * BLK), BF16)
-    keep, send = pl.pallas_call(
-        functools.partial(physics_kernel, (feats, hid, half, pad)),
-        out_shape=(t_shape, t_shape),
-        in_specs=[VMEM] * 4,
-        out_specs=(VMEM, VMEM),
-        compiler_params=PARAMS,
+    keep, send, before, after = pl.pallas_call(
+        functools.partial(physics_kernel, (feats, hid, half, pad, n_cells, n_role)),
+        out_shape=(t_shape, t_shape, halo_shape, halo_shape),
+        in_specs=[VMEM] * 5,
+        out_specs=(VMEM,) * 4,
+        scratch_shapes=[pltpu.VMEM(x_shape.shape, BF16), pltpu.SemaphoreType.DMA((2, 3))],
+        compiler_params=remote_params(1),
         cost_estimate=pl.CostEstimate(flops=2 * 10**9, bytes_accessed=4 * 10**6, transcendentals=10**6),
         name="physics",
-    )(x_own, x_other, mine, theirs)
+    )(x_own, x_send, packed, mine, theirs)
     got = lax.ppermute(send, "stack", swap)
 
     h_second = pl.pallas_call(

time: 106 us -> 94.8 us (0.89)
  Pallas kernels: 70.2 us -> 83.5 us
  starting transfers between devices: 10.9 us -> 0.95 us
  blocking collectives: 9.42 us -> 0 us
  local copies, waits for them, and re-layouts: 12.3 us -> 8.7 us
    pallas_call x2, Pallas kernels: 10.7 us -> 27.2 us  [the longest x1 14.5 us: body(): pl.pallas_call(functools.partial(open_kernel, (n_cells, n_role)), out_sha...]
    ppermute x5 -> x0, starting transfers between devices: 10.9 us -> none  [the longest x2 7.23 us: exchange(): after = lax.ppermute(packed[:margin], ring, down)]
    all_gather x1 -> x0, blocking collectives: 9.42 us -> none  [body(): wanted = lax.all_gather(recv_slot[0], 'cells')]
    slice x2 -> x0, local copies, waits for them, and re-layouts: 1.76 us -> none  [exchange(): after = lax.ppermute(packed[:margin], ring, down)]
    pallas_call x1, Pallas kernels: 31.6 us -> 29.9 us  [body(): pl.pallas_call(functools.partial(first_kernel, levels), out_shape=(shape(...]
    transpose x1 -> x0, local copies, waits for them, and re-layouts: 1.59 us -> none  [body(): v_rows = jnp.pad(jnp.concatenate([velocity, edge_coef[None]], axis=0), ((...]
    pallas_call x1, Pallas kernels: 25.8 us -> 24.2 us  [body(): pl.pallas_call(functools.partial(second_kernel, levels), out_shape=shape(...]
    unnamed x36 -> x20, local copies, waits for them, and re-layouts: 4.21 us -> 2.96 us
  transfers between devices with their start and end apart: 7 -> 2, of which waited for: 0 -> 0; matrix products, arithmetic and copies ran while one was open for 9% -> 3% of each run, Pallas kernels for 62% -> 73%
where the time goes in v2:
time: 94.8 us; the launch traced here: 94.5 us
  Pallas kernels  83.5 us (88%)
  local copies, waits for them, and re-layouts  8.7 us (9%)
  other arithmetic  1.18 us (1%)
  starting transfers between devices  0.95 us (1%)
    pallas_call x1, Pallas kernels, body(): pl.pallas_call(functools.partial(first_kernel, levels), out_shape=(shape(...  29.9 us
    pallas_call x1, Pallas kernels, body(): pl.pallas_call(functools.partial(second_kernel, levels), out_shape=shape(...  24.2 us
    pallas_call x1, Pallas kernels, body(): pl.pallas_call(functools.partial(open_kernel, (n_cells, n_role)), out_sha...  14.5 us
    pallas_call x1, Pallas kernels, body(): pl.pallas_call(functools.partial(physics_kernel, (feats, hid, half, pad,...  12.7 us
    unnamed x20, local copies, waits for them, and re-layouts  2.96 us
    pallas_call x1, Pallas kernels, body(): pl.pallas_call(close_kernel, out_shape=shape((levels, cells), F32), in_sp...  2.11 us
  transfers between devices with their start and end apart: 2, of which 0 were waited for; matrix products, arithmetic and copies ran while one was open for 3% of the time, Pallas kernels for 73%

profile of v2, /device:TPU:0, one launch (start us, length us, event | category | flops | bytes accessed | tf_op | source)
XLA Modules:
  0.0 94.5 jit_solution(11156814528764442762)
XLA Ops:
  0.0 0.8 reshape.79
  0.8 1.1 %copy.28 = bf16[512,256]{0,1:T(8,128)(2,1)S(1)} copy(bf16[512,256]{1,0:T(8,128)(2,1)} %param.29) | data formatting | bytes 524288 | tf_op args[13]
  1.9 0.8 broadcast_in_dim.36
  2.7 0.7 pad.26
  3.4 0.1 broadcast_in_dim.35
  3.5 1.2 %reshape.77 = bf16[45,10,512]{2,1,0:T(8,128)(2,1)S(1)} reshape(bf16[450,512]{1,0:T(8,128)(2,1)} %param.27) | data formatting | bytes 921600 | tf_op jit(solution)/shard_map/reshape | solution.py:326
  4.8 0.3 copy.29
  5.1 0.2 copy.25
  5.3 0.0 copy-start.3
  5.3 0.0 copy-start.2
  5.3 0.0 copy-start.7
  5.3 0.2 fusion.6
  5.5 0.1 fusion.4.p_own
  5.6 0.5 collective-permute-start
  6.1 0.6 broadcast_in_dim.29.edge_ref
  6.7 0.6 reshape.75.ec_ref
  7.4 0.6 pad.24.recv_ref
  8.0 14.5 %open_rows.1 = (f32[3072,128]{1,0:T(8,128)}, f32[4608,128]{1,0:T(8,128)}, bf16[256,128]{1,0:T(8,128)(2,1)}, bf16[256,128]{1,0:T(8,128)(2,1)}, s32[4,1,128]{2,1,0:T(1,128)}) custom-call(s32[512]{0:T(512)} %bitcast.17, f32[45,3072]{1,0:T(8,128)} %height_ref.1, f32[3,3072]{1,0:T(4,128)} %coef_ref.1, f32[45,4608]{1,0:T(8,128)} %velocity_ref.1, ...), custom_call_target="tpu_custom_call" | custom-call | tf_op jit(solution)/shard_map/open_rows/pallas_call | solution.py:304
  22.5 0.0 copy-start.4
  22.5 0.0 copy-start.8
  22.5 29.9 %first_substep.1 = (f32[3072,128]{1,0:T(8,128)}, f32[4608,128]{1,0:T(8,128)}, bf16[512,128]{1,0:T(8,128)(2,1)}, bf16[480,1024]{1,0:T(8,128)(2,1)}, bf16[480,1024]{1,0:T(8,128)(2,1)}) custom-call(s32[9216]{0:T(1024)} %reshape.75.ec_ref, s32[9216]{0:T(1024)} %bitcast.15, s32[512]{0:T(512)} %bitcast.18, s32[16]{0:T(128)} %bitcast.19, ...), custom_call_target="tpu_custom_call" | custom-call | tf_op jit(solution)/shard_map/first_substep/pallas_call | solution.py:350
  52.5 0.2 select_reduce_fusion
  52.7 0.2 and_reduce_fusion
  52.9 0.6 broadcast_select_fusion.count_ref
  53.4 0.0 collective-permute-done.p_other
  53.4 0.9 copy-done.6
  54.4 12.7 %physics.1 = (bf16[48,1024]{1,0:T(8,128)(2,1)}, bf16[48,1024]{1,0:T(8,128)(2,1)}, bf16[256,128]{1,0:T(8,128)(2,1)}, bf16[256,128]{1,0:T(8,128)(2,1)}) custom-call(bf16[480,1024]{1,0:T(8,128)(2,1)} %get-tuple-element.26.x_own, bf16[480,1024]{1,0:T(8,128)(2,1)} %get-tuple-element.27.x_mine, bf16[512,128]{1,0:T(8,128)(2,1)} %get-tuple-element.28.packed, ...), custom_call_target="tpu_custom_call" | custom-call | flops 2000000000 | bytes 4000000 | tf_op jit(solution)/shard_map/physics/pallas_call | solution.py:367
  67.1 0.4 collective-permute-start.1
  67.5 24.2 %second_substep.1.h_ref = f32[45,3072]{1,0:T(8,128)} custom-call(s32[9216]{0:T(1024)} %reshape.75.ec_ref, s32[9216]{0:T(1024)} %bitcast.16, f32[3072,128]{1,0:T(8,128)} %get-tuple-element.24.h_ref, f32[4608,128]{1,0:T(8,128)} %get-tuple-element.25.v_ref, bf16[256,128]{1,0:T(8,128)(2,1)} %get-tuple-element.29.before_ref, ...), custom_call_target="tpu_custom_call" | custom-call | flops 20000000000 | bytes 50000000 | tf_op jit(solution)/shard_map/second_substep/pallas_call | solution.py:379
  91.8 0.0 collective-permute-done.1.got_ref
  91.8 0.6 copy-done.1
  92.4 2.1 %close_add.1 = f32[45,3072]{1,0:T(8,128)} custom-call(s32[16]{0:T(128)} %bitcast.20, s32[16]{0:T(128)} %broadcast_select_fusion.count_ref, f32[45,3072]{1,0:T(8,128)} %second_substep.1.h_ref, bf16[48,1024]{1,0:T(8,128)(2,1)} %get-tuple-element.31.keep_ref, bf16[48,1024]{1,0:T(8,128)(2,1)} %copy-done.1), custom_call_target="tpu_custom_call" | custom-call | tf_op jit(solution)/shard_map/close_add/pallas_call | solution.py:390
  (16 shorter events, 0.1 us)
Async XLA Ops:
  5.3 0.8 copy-start.3
  5.3 1.4 %copy-start.2 = (s32[1,2,4608]{2,1,0:T(2,128)S(1)}, s32[1,2,4608]{2,1,0:T(2,128)}, u32[]{:S(2)}) copy-start(s32[1,2,4608]{2,1,0:T(2,128)} %param.22) | copy-start | bytes 110596
  5.3 2.0 %copy-start.7 = (s32[1,8]{1,0:T(1,128)S(1)}, s32[1,8]{1,0:T(1,128)}, u32[]{:S(2)}) copy-start(s32[1,8]{1,0:T(1,128)} %param.25) | copy-start | bytes 100
  5.6 46.9 %copy-start = (bf16[864,512]{1,0:T(8,128)(2,1)}, bf16[864,512]{1,0:T(8,128)(2,1)S(1)}, u32[]{:S(2)}) copy-start(bf16[864,512]{1,0:T(8,128)(2,1)S(1)} %fusion.4.p_own) | copy-start | bytes 2654212
  5.6 47.9 %collective-permute-start = (bf16[864,512]{1,0:T(8,128)(2,1)S(1)}, bf16[864,512]{1,0:T(8,128)(2,1)S(1)}, u32[]{:S(2)}, u32[]{:S(2)}) collective-permute-start(bf16[864,512]{1,0:T(8,128)(2,1)S(1)} %fusion.4.p_own), channel_id=1, source_target_pairs={{0,1},{1,0},{2,3},{3,2},{4,5},{5,4},{6,7},{7,6},{8,9},{9,8},{10,11... | collective-permute-start | bytes 2654216 | tf_op jit(solution)/shard_map/ppermute | solution.py:334
  22.5 30.0 %copy-start.4 = (s32[1,16]{1,0:T(1,128)S(1)}, s32[1,16]{1,0:T(1,128)}, u32[]{:S(2)}) copy-start(s32[1,16]{1,0:T(1,128)} %param.24) | copy-start | bytes 196
  22.5 30.0 %copy-start.8 = (s32[1,24]{1,0:T(1,128)S(1)}, s32[1,24]{1,0:T(1,128)}, u32[]{:S(2)}) copy-start(s32[1,24]{1,0:T(1,128)} %param.26) | copy-start | bytes 292
  22.5 30.2 %copy-start.5 = (s32[4,1,128]{2,1,0:T(1,128)S(1)}, s32[4,1,128]{2,1,0:T(1,128)}, u32[]{:S(2)}) copy-start(s32[4,1,128]{2,1,0:T(1,128)} %get-tuple-element.19) | copy-start | bytes 6148
  53.4 0.9 copy-start.6
  67.1 24.6 %collective-permute-start.1 = (bf16[48,1024]{1,0:T(8,128)(2,1)}, bf16[48,1024]{1,0:T(8,128)(2,1)S(1)}, u32[]{:S(2)}, u32[]{:S(2)}) collective-permute-start(bf16[48,1024]{1,0:T(8,128)(2,1)} %get-tuple-element.32), channel_id=1, source_target_pairs={{0,1},{1,0},{2,3},{3,2},{4,5},{5,4},{6,7},{7,6},{8,9},{9,8},{10,11... | collective-permute-start | bytes 294920 | tf_op jit(solution)/shard_map/ppermute | solution.py:377
  91.8 0.6 copy-start.1

commit v3 on v2

--- a/solution.py
+++ b/solution.py
@@ -91,9 +91,9 @@
 
 def to_rows(field_ref, extra_ref, rows_ref, wide):
     levels, count = field_ref.shape
-    extra = extra_ref.shape[0]
+    extra = extra_ref[...].reshape(-1, count)
     wide[0:levels, 0:count] = field_ref[...]
-    wide[levels : levels + extra, 0:count] = extra_ref[...]
+    wide[levels : levels + extra.shape[0], 0:count] = extra
     for b in range(count // BLK):
         cols = slice(b * BLK, (b + 1) * BLK)
         rows_ref[cols, :] = wide[:, cols].T
@@ -220,11 +220,25 @@
         out_ref[:, at] = (h - div).T[0:levels, :]
 
 
+def by_quantity(w_ref, nq, pad):
+    rows, hid = w_ref.shape
+    levels = rows // nq
+    level = lax.broadcasted_iota(jnp.int32, (pad, rows), 0)
+    entry = lax.broadcasted_iota(jnp.int32, (pad, rows), 1)
+    parts = []
+    for q in range(nq):
+        chosen = (entry == level * nq + q) & (level < levels)
+        chosen = jnp.where(chosen, 1.0, 0.0).astype(BF16)
+        parts.append(jnp.dot(chosen, w_ref[...], preferred_element_type=F32).T)
+    return jnp.concatenate(parts, axis=1).astype(BF16)
+
+
 def physics_kernel(
-    sizes, x_own, x_mine, packed, p_own, p_other,
-    keep_ref, send_ref, before_ref, after_ref, x_other, sems,
+    sizes, x_own, x_mine, packed, bias_one, *refs
 ):
-    feats, hid, half, pad, n_cells, n_role = sizes
+    weights, refs = refs[:8], refs[8:]
+    keep_ref, send_ref, before_ref, after_ref, x_other, first, sems = refs
+    nq, pad, n_cells, n_role = sizes
     me = lax.axis_index("stack")
     ring = around_ring(n_cells, n_role)
     twin = {"stack": 1 - me}
@@ -233,28 +247,35 @@
     swap = remote(x_mine, x_other, sems, 2, twin)
     for copy in [swap] + halos:
         copy.start()
+    ours, theirs = weights[:4], weights[4:]
+    first[0] = by_quantity(ours[0], nq, pad)
+    first[1] = by_quantity(theirs[0], nq, pad)
     swap.wait()
-    bias_one = p_own[0:hid, feats + 1 : feats + 2].astype(F32)
 
     def dot(a, b):
         return jnp.dot(a, b, preferred_element_type=F32)
 
+    def across(a, b):
+        return lax.dot_general(a, b, (((0,), (0,)), ((), ())), preferred_element_type=F32)
+
     def silu(v):
         return (v / (1.0 + jnp.exp(-v))).astype(BF16)
 
-    for base in range(0, x_own.shape[1], 256):
-        at = slice(base, base + 256)
-        one = dot(p_own[0:hid, 0:feats], x_own[:, at]) + dot(p_other[0:hid, 0:feats], x_other[:, at])
-        one = silu(one + bias_one)
-        twos = []
-        for p in (p_own, p_other):
-            bias_two = p[0:half, feats : feats + 1].astype(F32)
-            twos.append(silu(dot(p[hid : hid + half, :], one) + bias_two))
-        for ref, which in ((keep_ref, me), (send_ref, 1 - me)):
-            start = pl.multiple_of(hid + half + which * pad, 16)
-            total = dot(p_own[pl.ds(start, pad), 0:half], twos[0])
-            total += dot(p_other[pl.ds(start, pad), 0:half], twos[1])
-            ref[:, at] = total.astype(BF16)
+    chunk = 256
+    levels = ours[2].shape[1] // 2
+    ones = jnp.ones((1, chunk), BF16)
+    for base in range(0, x_own.shape[1], chunk):
+        at = slice(base, base + chunk)
+        one = dot(first[0], x_own[:, at]) + dot(first[1], x_other[:, at])
+        one = silu(one + across(bias_one[...], ones))
+        total = None
+        for _, second, third, bias in (ours, theirs):
+            two = silu(across(second[...], one) + across(bias[...], ones))
+            term = across(third[...], two)
+            total = term if total is None else total + term
+        low, high = total[0:levels], total[levels : 2 * levels]
+        keep_ref[:, at] = jnp.where(me == 0, low, high).astype(BF16).astype(F32)
+        send_ref[0:levels, at] = jnp.where(me == 0, high, low).astype(BF16)
     for copy in halos:
         copy.wait()
 
@@ -264,15 +285,15 @@
     me = lax.axis_index("stack")
     half = sb_ref.shape[0] // 2
     out_ref[...] = h_ref[...]
-    lane = lax.broadcasted_iota(jnp.int32, (keep_ref.shape[0], BLK), 1)
+    lane = lax.broadcasted_iota(jnp.int32, (levels, BLK), 1)
     for which, ref in ((me, keep_ref), (1 - me, got_ref)):
         for j in range(half):
             s = which * half + j
             b = jnp.maximum(sb_ref[s], 0)
             at = pl.ds(pl.multiple_of(b * BLK, BLK), BLK)
-            tend = ref[:, j * BLK : (j + 1) * BLK].astype(F32)
+            tend = ref[:, j * BLK : (j + 1) * BLK].astype(F32)[0:levels, :]
             tend = jnp.where(lane < count_ref[s], tend, 0.0)
-            out_ref[:, at] = out_ref[:, at] + tend[0:levels, :]
+            out_ref[:, at] = out_ref[:, at] + tend
 
 
 def body(
@@ -289,7 +310,6 @@
     nq = NDER + tracers.shape[0]
     pad = up16(levels + 3)
     feats = nq * pad
-    hid, half = w_second.shape
     swap = [(0, 1), (1, 0)]
     halo = halo_send.reshape(-1)
     ec = edge_cells.reshape(-1)
@@ -299,6 +319,8 @@
     def shape(dims, dtype):
         return jax.ShapeDtypeStruct(dims, dtype)
 
+    ours = (w_first, w_second, w_third, b_second[None])
+    theirs = tuple(lax.ppermute(array, "stack", swap) for array in ours)
     halo_shape = shape((margin, LANES), BF16)
     recv = jnp.pad(recv_slot, ((0, 0), (0, LANES - recv_slot.shape[1])), constant_values=-1)
     h_rows, v_rows, before, after, wanted = pl.pallas_call(
@@ -320,18 +342,8 @@
         ],
         compiler_params=remote_params(0),
         name="open_rows",
-    )(halo, height, cell_coef, velocity, edge_coef[None], recv)
+    )(halo, height, cell_coef, velocity, edge_coef, recv)
     wanted = wanted.reshape(n_cells, LANES)
-
-    one = w_first.reshape(levels, nq, hid).transpose(2, 1, 0)
-    one = jnp.pad(one, ((0, 0), (0, 0), (0, pad - levels))).reshape(hid, feats)
-    bias_two = jnp.pad(b_second, (0, hid - half))
-    one = jnp.concatenate([one, bias_two[:, None], b_first[:, None]], axis=1)
-    one = jnp.pad(one, ((0, 0), (0, hid - one.shape[1])))
-    three = jnp.pad(w_third.T.reshape(2, levels, half), ((0, 0), (0, pad - levels), (0, 0)))
-    three = jnp.pad(three.reshape(2 * pad, half), ((0, 0), (0, hid - half)))
-    mine = jnp.concatenate([one, w_second.T, three], axis=0)
-    theirs = lax.ppermute(mine, "stack", swap)
 
     slot = jnp.arange(slots, dtype=jnp.int32)
     entry = lax.axis_index("cells") * cap + slot % cap
@@ -363,17 +375,21 @@
         name="first_substep",
     )(ec, ce, halo, sb, h_rows, v_rows, before, after, tracers)
 
-    t_shape = shape((pad, half_slots * BLK), BF16)
+    width = half_slots * BLK
     keep, send, before, after = pl.pallas_call(
-        functools.partial(physics_kernel, (feats, hid, half, pad, n_cells, n_role)),
-        out_shape=(t_shape, t_shape, halo_shape, halo_shape),
-        in_specs=[VMEM] * 5,
+        functools.partial(physics_kernel, (nq, pad, n_cells, n_role)),
+        out_shape=(shape((levels, width), F32), shape((pad, width), BF16), halo_shape, halo_shape),
+        in_specs=[VMEM] * 12,
         out_specs=(VMEM,) * 4,
-        scratch_shapes=[pltpu.VMEM(x_shape.shape, BF16), pltpu.SemaphoreType.DMA((2, 3))],
+        scratch_shapes=[
+            pltpu.VMEM(x_shape.shape, BF16),
+            pltpu.VMEM((2, w_first.shape[1], feats), BF16),
+            pltpu.SemaphoreType.DMA((2, 3)),
+        ],
         compiler_params=remote_params(1),
         cost_estimate=pl.CostEstimate(flops=2 * 10**9, bytes_accessed=4 * 10**6, transcendentals=10**6),
         name="physics",
-    )(x_own, x_send, packed, mine, theirs)
+    )(x_own, x_send, packed, b_first[None], *ours, *theirs)
     got = lax.ppermute(send, "stack", swap)
 
     h_second = pl.pallas_call(

time: 94.8 us -> 94.4 us (level)
  local copies, waits for them, and re-layouts: 8.7 us -> 6.22 us
  other arithmetic: 1.18 us -> 2.25 us
    reshape x3 -> x0, local copies, waits for them, and re-layouts: 2.23 us -> none  [the longest x1 1.21 us: body(): one = w_first.reshape(levels, nq, hid).transpose(2, 1, 0)]
    unnamed x20 -> x17, local copies, waits for them, and re-layouts: 2.96 us -> 2.4 us
  transfers between devices with their start and end apart: 2 -> 5, of which waited for: 0 -> 0; matrix products, arithmetic and copies ran while one was open for 3% -> 7% of each run, Pallas kernels for 73% -> 73%
where the time goes in v3:
time: 94.4 us; the launch traced here: 94 us
  Pallas kernels  84.2 us (89%)
  local copies, waits for them, and re-layouts  6.22 us (7%)
  other arithmetic  2.25 us (2%)
  starting transfers between devices  1.16 us (1%)
    pallas_call x1, Pallas kernels, body(): pl.pallas_call(functools.partial(first_kernel, levels), out_shape=(shape(...  30 us
    pallas_call x1, Pallas kernels, body(): pl.pallas_call(functools.partial(second_kernel, levels), out_shape=shape(...  24.2 us
    pallas_call x1, Pallas kernels, body(): pl.pallas_call(functools.partial(open_kernel, (n_cells, n_role)), out_sha...  14.6 us
    pallas_call x1, Pallas kernels, body(): pl.pallas_call(functools.partial(physics_kernel, (nq, pad, n_cells, n_rol...  13.3 us
    unnamed x17, local copies, waits for them, and re-layouts  2.4 us
    pallas_call x1, Pallas kernels, body(): pl.pallas_call(close_kernel, out_shape=shape((levels, cells), F32), in_sp...  2.14 us
  transfers between devices with their start and end apart: 5, of which 0 were waited for; matrix products, arithmetic and copies ran while one was open for 7% of the time, Pallas kernels for 73%

profile of v3, /device:TPU:0, one launch (start us, length us, event | category | flops | bytes accessed | tf_op | source)
XLA Modules:
  0.0 94.0 jit_solution(6580614131075199141)
XLA Ops:
  0.0 0.5 collective-permute-start
  0.5 0.1 collective-permute-start.1
  0.5 0.9 copy.20.refs_2_
  1.4 0.5 collective-permute-start.2
  2.0 0.7 broadcast_in_dim.30.refs_3_
  2.6 0.1 collective-permute-start.3
  2.7 1.2 %pad.4.recv_ref = s32[1,128]{1,0:T(1,128)} pad(s32[1,8]{1,0:T(1,128)} %param.25, s32[]{:T(128)} %constant.31.clone.1), padding=0_0x0_120 | pad | bytes 548 | tf_op jit(solution)/shard_map/jit(_pad)/pad | solution.py:325
  3.9 14.6 %open_rows.1 = (f32[3072,128]{1,0:T(8,128)}, f32[4608,128]{1,0:T(8,128)}, bf16[256,128]{1,0:T(8,128)(2,1)}, bf16[256,128]{1,0:T(8,128)(2,1)}, s32[4,1,128]{2,1,0:T(1,128)}) custom-call(s32[512]{0:T(512)} %bitcast.7, f32[45,3072]{1,0:T(8,128)} %height_ref.1, f32[3,3072]{1,0:T(4,128)} %coef_ref.1, f32[45,4608]{1,0:T(8,128)} %velocity_ref.1, f32[4608]{0:T(1024)} %edge_ref.1, ...), custom_call_target="tpu_custom_call" | custom-call | tf_op jit(solution)/shard_map/open_rows/pallas_call | solution.py:326
  18.4 0.9 and_reduce_fusion
  19.3 0.9 select_reduce_fusion
  20.2 0.5 broadcast_select_fusion.count_ref
  20.7 1.4 %reshape.63.ec_ref = s32[9216]{0:T(1024)} reshape(s32[1,2,4608]{2,1,0:T(2,128)} %param.22) | data formatting | bytes 73728 | tf_op jit(solution)/shard_map/reshape | solution.py:315
  22.1 0.0 copy-done.2
  22.1 0.6 broadcast_in_dim.29.bias_one
  22.7 30.0 %first_substep.1 = (f32[3072,128]{1,0:T(8,128)}, f32[4608,128]{1,0:T(8,128)}, bf16[512,128]{1,0:T(8,128)(2,1)}, bf16[480,1024]{1,0:T(8,128)(2,1)}, bf16[480,1024]{1,0:T(8,128)(2,1)}) custom-call(s32[9216]{0:T(1024)} %reshape.63.ec_ref, s32[9216]{0:T(1024)} %bitcast.5, s32[512]{0:T(512)} %bitcast.8, s32[16]{0:T(128)} %bitcast.10, ...), custom_call_target="tpu_custom_call" | custom-call | tf_op jit(solution)/shard_map/first_substep/pallas_call | solution.py:362
  52.6 0.0 copy-done.1
  52.6 0.0 collective-permute-done.3.refs_7_
  52.7 0.0 collective-permute-done.2.refs_6_
  52.7 0.0 collective-permute-done.1.refs_5_
  52.7 0.0 copy-start.4
  52.7 0.0 collective-permute-done.refs_4_
  52.7 0.0 copy-start.3
  52.7 0.5 copy-done.7
  53.2 0.1 copy-done.5
  53.3 0.1 copy-done.4
  53.4 0.1 copy-done.3
  53.6 13.3 %physics.1 = (f32[45,1024]{1,0:T(8,128)}, bf16[48,1024]{1,0:T(8,128)(2,1)}, bf16[256,128]{1,0:T(8,128)(2,1)}, bf16[256,128]{1,0:T(8,128)(2,1)}) custom-call(bf16[480,1024]{1,0:T(8,128)(2,1)} %get-tuple-element.26.x_own, bf16[480,1024]{1,0:T(8,128)(2,1)} %get-tuple-element.27.x_mine, bf16[512,128]{1,0:T(8,128)(2,1)} %get-tuple-element.28.packed, ...), custom_call_target="tpu_custom_call" | custom-call | flops 2000000000 | bytes 4000000 | tf_op jit(solution)/shard_map/physics/pallas_call | solution.py:379
  66.9 0.1 collective-permute-start.4
  67.0 24.2 %second_substep.1.h_ref = f32[45,3072]{1,0:T(8,128)} custom-call(s32[9216]{0:T(1024)} %reshape.63.ec_ref, s32[9216]{0:T(1024)} %bitcast.6, f32[3072,128]{1,0:T(8,128)} %get-tuple-element.24.h_ref, f32[4608,128]{1,0:T(8,128)} %get-tuple-element.25.v_ref, bf16[256,128]{1,0:T(8,128)(2,1)} %get-tuple-element.29.before_ref, ...), custom_call_target="tpu_custom_call" | custom-call | flops 20000000000 | bytes 50000000 | tf_op jit(solution)/shard_map/second_substep/pallas_call | solution.py:395
  91.2 0.0 collective-permute-done.4.got_ref
  91.2 0.6 copy-done
  91.8 2.1 %close_add.1 = f32[45,3072]{1,0:T(8,128)} custom-call(s32[16]{0:T(128)} %bitcast.11, s32[16]{0:T(128)} %broadcast_select_fusion.count_ref, f32[45,3072]{1,0:T(8,128)} %second_substep.1.h_ref, f32[45,1024]{1,0:T(8,128)} %get-tuple-element.31.keep_ref, bf16[48,1024]{1,0:T(8,128)(2,1)} %copy-done), custom_call_target="tpu_custom_call" | custom-call | tf_op jit(solution)/shard_map/close_add/pallas_call | solution.py:406
  (10 shorter events, 0.0 us)
Async XLA Ops:
  0.0 22.1 %copy-start.2 = (bf16[512]{0:T(512)(128)(2,1)S(1)}, bf16[512]{0:T(512)(128)(2,1)}, u32[]{:S(2)}) copy-start(bf16[512]{0:T(512)(128)(2,1)} %param.28) | copy-start | bytes 3076
  0.0 52.7 %collective-permute-start = (bf16[450,512]{1,0:T(8,128)(2,1)}, bf16[450,512]{1,0:T(8,128)(2,1)S(1)}, u32[]{:S(2)}, u32[]{:S(2)}) collective-permute-start(bf16[450,512]{1,0:T(8,128)(2,1)} %refs_0_.1), channel_id=1, source_target_pairs={{0,1},{1,0},{2,3},{3,2},{4,5},{5,4},{6,7},{7,6},{8,9},{9,8},{10,11... | collective-permute-start | bytes 1382408 | tf_op jit(solution)/shard_map/ppermute | solution.py:323
  0.5 52.2 %collective-permute-start.1 = (bf16[512,256]{1,0:T(8,128)(2,1)}, bf16[512,256]{1,0:T(8,128)(2,1)S(1)}, u32[]{:S(2)}, u32[]{:S(2)}) collective-permute-start(bf16[512,256]{1,0:T(8,128)(2,1)} %refs_1_.1), channel_id=1, source_target_pairs={{0,1},{1,0},{2,3},{3,2},{4,5},{5,4},{6,7},{7,6},{8,9},{9,8},{10,11... | collective-permute-start | bytes 786440 | tf_op jit(solution)/shard_map/ppermute | solution.py:323
  1.4 51.2 %copy-start.1 = (bf16[256,90]{1,0:T(8,128)(2,1)}, bf16[256,90]{1,0:T(8,128)(2,1)S(1)}, u32[]{:S(2)}) copy-start(bf16[256,90]{1,0:T(8,128)(2,1)S(1)} %copy.20.refs_2_) | copy-start | bytes 138244
  1.4 51.2 %collective-permute-start.2 = (bf16[256,90]{1,0:T(8,128)(2,1)S(1)}, bf16[256,90]{1,0:T(8,128)(2,1)S(1)}, u32[]{:S(2)}, u32[]{:S(2)}) collective-permute-start(bf16[256,90]{1,0:T(8,128)(2,1)S(1)} %copy.20.refs_2_), channel_id=1, source_target_pairs={{0,1},{1,0},{2,3},{3,2},{4,5},{5,4},{6,7},{7,6},{8,9},{9,8},{10,11... | collective-permute-start | bytes 138248 | tf_op jit(solution)/shard_map/ppermute | solution.py:323
  2.6 50.0 %copy-start.6 = (bf16[1,256]{1,0:T(2,128)(2,1)}, bf16[1,256]{1,0:T(2,128)(2,1)S(1)}, u32[]{:S(2)}) copy-start(bf16[1,256]{1,0:T(2,128)(2,1)S(1)} %broadcast_in_dim.30.refs_3_) | copy-start | bytes 1540
  2.6 50.0 %collective-permute-start.3 = (bf16[1,256]{1,0:T(2,128)(2,1)S(1)}, bf16[1,256]{1,0:T(2,128)(2,1)S(1)}, u32[]{:S(2)}, u32[]{:S(2)}) collective-permute-start(bf16[1,256]{1,0:T(2,128)(2,1)S(1)} %broadcast_in_dim.30.refs_3_), channel_id=1, source_target_pairs={{0,1},{1,0},{2,3},{3,2},{4,5},{5,4},{6,7},{7,6},{8,9},{9,8},{10,11... | collective-permute-start | bytes 1544 | tf_op jit(solution)/shard_map/ppermute | solution.py:323
  52.7 0.6 copy-start.7
  52.7 0.6 copy-start.5
  52.7 0.7 copy-start.4
  52.7 0.8 copy-start.3
  66.9 24.3 %collective-permute-start.4 = (bf16[48,1024]{1,0:T(8,128)(2,1)}, bf16[48,1024]{1,0:T(8,128)(2,1)S(1)}, u32[]{:S(2)}, u32[]{:S(2)}) collective-permute-start(bf16[48,1024]{1,0:T(8,128)(2,1)} %get-tuple-element.32), channel_id=1, source_target_pairs={{0,1},{1,0},{2,3},{3,2},{4,5},{5,4},{6,7},{7,6},{8,9},{9,8},{10,11... | collective-permute-start | bytes 294920 | tf_op jit(solution)/shard_map/ppermute | solution.py:393
  91.2 0.6 copy-start

commit v4 on v3

--- a/solution.py
+++ b/solution.py
@@ -125,18 +125,20 @@
         copy.wait()
 
 
-def edges_and_cells(levels, ec_ref, ce_ref, h_ref, v_ref, before_ref, after_ref, v_out, ext, dif, beside):
-    cells, edges = h_ref.shape[0], v_ref.shape[0]
+def fill_rims(ext, cells, before_ref, after_ref):
     margin = before_ref.shape[0]
-    ext[0:cells, :] = h_ref[...]
     ext[cells : cells + margin, :] = before_ref[...].astype(F32)
     ext[cells + margin : cells + 2 * margin, :] = after_ref[...].astype(F32)
 
+
+def edge_part(levels, ec_ref, v_ref, v_out, ext, dif):
+    edges = v_ref.shape[0]
+
     def some_edges(base):
+        place = base + base // LANES * LANES
         found = []
         for u in range(32):
-            e = base + u
-            found.append(row(ext, ec_ref[edges + e]) - row(ext, ec_ref[e]))
+            found.append(row(ext, ec_ref[place + LANES + u]) - row(ext, ec_ref[place + u]))
         for u in range(32):
             dif[pl.ds(base + u, 1), :] = found[u]
 
@@ -150,11 +152,15 @@
 
     loop(edges, 128, move)
 
+
+def cell_part(ce_ref, moved, beside):
+    cells = beside.shape[1]
+
     def some_cells(base):
         found = []
         for u in range(16):
             for k in range(3):
-                found.append((u, k, row(v_out, ce_ref[k * cells + base + u])))
+                found.append((u, k, row(moved, ce_ref[k * cells + base + u])))
         for u, k, value in found:
             beside[k, pl.ds(base + u, 1), :] = value
 
@@ -173,8 +179,11 @@
     levels, ec_ref, ce_ref, halo_ref, sb_ref, h_ref, v_ref, before_ref, after_ref, tr_ref,
     h_out, v_out, pack_out, own_ref, other_ref, ext, dif, beside, stage,
 ):
-    edges_and_cells(levels, ec_ref, ce_ref, h_ref, v_ref, before_ref, after_ref, v_out, ext, dif, beside)
     cells = h_ref.shape[0]
+    ext[0:cells, :] = h_ref[...]
+    fill_rims(ext, cells, before_ref, after_ref)
+    edge_part(levels, ec_ref, v_ref, v_out, ext, dif)
+    cell_part(ce_ref, v_out, beside)
     pad = own_ref.shape[0] // (NDER + tr_ref.shape[0])
 
     def move(base):
@@ -211,15 +220,6 @@
                 x_ref[q * pad : q * pad + levels, cols] = tr_ref[t, :, at]
 
 
-def second_kernel(levels, ec_ref, ce_ref, h_ref, v_ref, before_ref, after_ref, out_ref, moved, ext, dif, beside):
-    edges_and_cells(levels, ec_ref, ce_ref, h_ref, v_ref, before_ref, after_ref, moved, ext, dif, beside)
-    for b in range(h_ref.shape[0] // BLK):
-        at = slice(b * BLK, (b + 1) * BLK)
-        h = h_ref[at, :]
-        div = spread_of(levels, h, beside[0, at, :], beside[1, at, :], beside[2, at, :])
-        out_ref[:, at] = (h - div).T[0:levels, :]
-
-
 def by_quantity(w_ref, nq, pad):
     rows, hid = w_ref.shape
     levels = rows // nq
@@ -233,24 +233,45 @@
     return jnp.concatenate(parts, axis=1).astype(BF16)
 
 
-def physics_kernel(
-    sizes, x_own, x_mine, packed, bias_one, *refs
-):
+def second_kernel(sizes, ec_ref, ce_ref, h_ref, v_ref, x_own, x_mine, packed, bias_one, *refs):
     weights, refs = refs[:8], refs[8:]
-    keep_ref, send_ref, before_ref, after_ref, x_other, first, sems = refs
+    out_ref, keep_ref, got_ref, x_other, before, after, send, first, sems, moved, ext, dif, beside = refs
     nq, pad, n_cells, n_role = sizes
+    cells = h_ref.shape[0]
+    levels = out_ref.shape[0]
     me = lax.axis_index("stack")
     ring = around_ring(n_cells, n_role)
     twin = {"stack": 1 - me}
     greet(ring + [twin])
-    halos = halo_copies(packed, before_ref, after_ref, sems, ring)
+    halos = halo_copies(packed, before, after, sems, ring)
     swap = remote(x_mine, x_other, sems, 2, twin)
-    for copy in [swap] + halos:
+    for copy in halos + [swap]:
         copy.start()
     ours, theirs = weights[:4], weights[4:]
     first[0] = by_quantity(ours[0], nq, pad)
     first[1] = by_quantity(theirs[0], nq, pad)
+    ext[0:cells, :] = h_ref[...]
+    send[...] = jnp.zeros_like(send)
+    for copy in halos:
+        copy.wait()
+    fill_rims(ext, cells, before, after)
+    edge_part(levels, ec_ref, v_ref, moved, ext, dif)
     swap.wait()
+    physics((x_own, x_other), first, bias_one, (ours, theirs), keep_ref, send)
+    back = remote(send, got_ref, sems, 3, twin)
+    back.start()
+    cell_part(ce_ref, moved, beside)
+    for b in range(cells // BLK):
+        at = slice(b * BLK, (b + 1) * BLK)
+        h = h_ref[at, :]
+        div = spread_of(levels, h, beside[0, at, :], beside[1, at, :], beside[2, at, :])
+        out_ref[:, at] = (h - div).T[0:levels, :]
+    back.wait()
+
+
+def physics(inputs, first, bias_one, weights, keep_ref, send_ref):
+    me = lax.axis_index("stack")
+    x_own, x_other = inputs
 
     def dot(a, b):
         return jnp.dot(a, b, preferred_element_type=F32)
@@ -262,26 +283,27 @@
         return (v / (1.0 + jnp.exp(-v))).astype(BF16)
 
     chunk = 256
-    levels = ours[2].shape[1] // 2
+    levels = keep_ref.shape[0]
     ones = jnp.ones((1, chunk), BF16)
     for base in range(0, x_own.shape[1], chunk):
         at = slice(base, base + chunk)
         one = dot(first[0], x_own[:, at]) + dot(first[1], x_other[:, at])
         one = silu(one + across(bias_one[...], ones))
         total = None
-        for _, second, third, bias in (ours, theirs):
+        for _, second, third, bias in weights:
             two = silu(across(second[...], one) + across(bias[...], ones))
             term = across(third[...], two)
             total = term if total is None else total + term
         low, high = total[0:levels], total[levels : 2 * levels]
         keep_ref[:, at] = jnp.where(me == 0, low, high).astype(BF16).astype(F32)
         send_ref[0:levels, at] = jnp.where(me == 0, high, low).astype(BF16)
-    for copy in halos:
-        copy.wait()
-
-
-def close_kernel(sb_ref, count_ref, h_ref, keep_ref, got_ref, out_ref):
+
+
+def close_kernel(sb_ref, live_ref, wanted_ref, h_ref, keep_ref, got_ref, out_ref):
     levels = h_ref.shape[0]
+    slots = sb_ref.shape[0]
+    cap = slots // wanted_ref.shape[0]
+    here = lax.axis_index("cells") * cap
     me = lax.axis_index("stack")
     half = sb_ref.shape[0] // 2
     out_ref[...] = h_ref[...]
@@ -292,7 +314,13 @@
             b = jnp.maximum(sb_ref[s], 0)
             at = pl.ds(pl.multiple_of(b * BLK, BLK), BLK)
             tend = ref[:, j * BLK : (j + 1) * BLK].astype(F32)[0:levels, :]
-            tend = jnp.where(lane < count_ref[s], tend, 0.0)
+            dest = lax.div(s, cap)
+            entry = here + lax.rem(s, cap)
+            uses = jnp.int32(0)
+            for i in range(wanted_ref.shape[1]):
+                uses += (wanted_ref[dest, i] == entry).astype(jnp.int32)
+            live = jnp.where((uses > 0) & (sb_ref[s] >= 0), live_ref[b], 0)
+            tend = jnp.where(lane < live, tend, 0.0)
             out_ref[:, at] = out_ref[:, at] + tend
 
 
@@ -306,13 +334,12 @@
     margin = halo_send.shape[1] // 2
     slots = send_block.shape[1]
     half_slots = slots // 2
-    cap = slots // n_cells
     nq = NDER + tracers.shape[0]
     pad = up16(levels + 3)
     feats = nq * pad
     swap = [(0, 1), (1, 0)]
     halo = halo_send.reshape(-1)
-    ec = edge_cells.reshape(-1)
+    ec = edge_cells.reshape(2, edges // LANES, LANES).transpose(1, 0, 2).reshape(-1)
     ce = cell_edges.reshape(-1)
     sb = send_block.reshape(-1)
 
@@ -343,15 +370,7 @@
         compiler_params=remote_params(0),
         name="open_rows",
     )(halo, height, cell_coef, velocity, edge_coef, recv)
-    wanted = wanted.reshape(n_cells, LANES)
-
-    slot = jnp.arange(slots, dtype=jnp.int32)
-    entry = lax.axis_index("cells") * cap + slot % cap
-    dest = jnp.arange(wanted.shape[0], dtype=jnp.int32)
-    match = (wanted[None] == entry[:, None, None]) & (dest[None, :, None] == (slot // cap)[:, None, None])
-    block = jnp.arange(cells // BLK, dtype=jnp.int32)
-    counts = jnp.sum(jnp.where(sb[:, None] == block[None], block_count[0][None], 0), axis=1)
-    counts = jnp.where(jnp.any(match, axis=(1, 2)), counts, 0).astype(jnp.int32)
+    wanted = wanted[:, 0, : recv_slot.shape[1]]
 
     field_scratch = [
         pltpu.VMEM((cells + 2 * margin, LANES), F32),
@@ -376,41 +395,34 @@
     )(ec, ce, halo, sb, h_rows, v_rows, before, after, tracers)
 
     width = half_slots * BLK
-    keep, send, before, after = pl.pallas_call(
-        functools.partial(physics_kernel, (nq, pad, n_cells, n_role)),
-        out_shape=(shape((levels, width), F32), shape((pad, width), BF16), halo_shape, halo_shape),
-        in_specs=[VMEM] * 12,
-        out_specs=(VMEM,) * 4,
+    t_shape = shape((pad, width), BF16)
+    h_second, keep, got = pl.pallas_call(
+        functools.partial(second_kernel, (nq, pad, n_cells, n_role)),
+        out_shape=(shape((levels, cells), F32), shape((levels, width), F32), t_shape),
+        in_specs=[SMEM] * 2 + [VMEM] * 14,
+        out_specs=(VMEM,) * 3,
         scratch_shapes=[
             pltpu.VMEM(x_shape.shape, BF16),
+            pltpu.VMEM(halo_shape.shape, BF16),
+            pltpu.VMEM(halo_shape.shape, BF16),
+            pltpu.VMEM(t_shape.shape, BF16),
             pltpu.VMEM((2, w_first.shape[1], feats), BF16),
-            pltpu.SemaphoreType.DMA((2, 3)),
-        ],
+            pltpu.SemaphoreType.DMA((2, 4)),
+            pltpu.VMEM((edges, LANES), F32),
+        ]
+        + field_scratch,
         compiler_params=remote_params(1),
-        cost_estimate=pl.CostEstimate(flops=2 * 10**9, bytes_accessed=4 * 10**6, transcendentals=10**6),
-        name="physics",
-    )(x_own, x_send, packed, b_first[None], *ours, *theirs)
-    got = lax.ppermute(send, "stack", swap)
-
-    h_second = pl.pallas_call(
-        functools.partial(second_kernel, levels),
-        out_shape=shape((levels, cells), F32),
-        in_specs=[SMEM] * 2 + [VMEM] * 4,
-        out_specs=VMEM,
-        scratch_shapes=[pltpu.VMEM((edges, LANES), F32)] + field_scratch,
-        compiler_params=PARAMS,
-        cost_estimate=pl.CostEstimate(flops=2 * 10**10, bytes_accessed=50 * 10**6, transcendentals=0),
         name="second_substep",
-    )(ec, ce, h_rows, v_rows, before, after)
+    )(ec, ce, h_rows, v_rows, x_own, x_send, packed, b_first[None], *ours, *theirs)
 
     return pl.pallas_call(
         close_kernel,
         out_shape=shape((levels, cells), F32),
-        in_specs=[SMEM] * 2 + [VMEM] * 3,
+        in_specs=[SMEM] * 3 + [VMEM] * 3,
         out_specs=VMEM,
         compiler_params=PARAMS,
         name="close_add",
-    )(sb, counts, h_second, keep, got)
+    )(sb, block_count.reshape(-1), wanted, h_second, keep, got)
 
 
 def solution(mesh):

time: 94.4 us -> 93.4 us (0.989)
  other arithmetic: 2.25 us -> 0 us
  Pallas kernels: 84.2 us -> 85.6 us
    unnamed x17 -> x13, local copies, waits for them, and re-layouts: 2.4 us -> 1.76 us
    pallas_call x2 -> x1, Pallas kernels: 37.6 us -> 37.9 us  [body(): pl.pallas_call(functools.partial(second_kernel, (nq, pad, n_cells, n_role...]
  transfers between devices with their start and end apart: 5 -> 4, of which waited for: 0 -> 0; matrix products, arithmetic and copies ran while one was open for 7% -> 6% of each run, Pallas kernels for 73% -> 49%
where the time goes in v4:
time: 93.4 us; the launch traced here: 93.1 us
  Pallas kernels  85.6 us (92%)
  local copies, waits for them, and re-layouts  6.27 us (7%)
  starting transfers between devices  1.09 us (1%)
    pallas_call x1, Pallas kernels, body(): pl.pallas_call(functools.partial(second_kernel, (nq, pad, n_cells, n_role...  37.9 us
    pallas_call x1, Pallas kernels, body(): pl.pallas_call(functools.partial(first_kernel, levels), out_shape=(shape(...  30.8 us
    pallas_call x1, Pallas kernels, body(): pl.pallas_call(functools.partial(open_kernel, (n_cells, n_role)), out_sha...  14.5 us
    pallas_call x1, Pallas kernels, body(): pl.pallas_call(close_kernel, out_shape=shape((levels, cells), F32), in_sp...  2.31 us
  transfers between devices with their start and end apart: 4, of which 0 were waited for; matrix products, arithmetic and copies ran while one was open for 6% of the time, Pallas kernels for 49%

profile of v4, /device:TPU:0, one launch (start us, length us, event | category | flops | bytes accessed | tf_op | source)
XLA Modules:
  0.0 93.1 jit_solution(6217603416809127607)
XLA Ops:
  0.0 0.5 collective-permute-start
  0.5 0.1 collective-permute-start.1
  0.5 0.9 copy.21.refs_2_
  1.4 0.0 copy-start.1
  1.4 0.5 collective-permute-start.2
  2.0 0.7 broadcast_in_dim.7.refs_3_
  2.6 0.0 copy-start.4
  2.6 0.1 collective-permute-start.3
  2.7 0.8 reshape.21
  3.5 0.6 copy.19
  4.1 1.3 %broadcast_in_dim.6.bias_one = bf16[1,512]{1,0:T(2,128)(2,1)} reshape(bf16[512]{0:T(512)(128)(2,1)} %param.28) | data formatting | bytes 2048 | tf_op jit(solution)/shard_map/broadcast_in_dim | solution.py:416
  5.4 1.2 %pad.4.recv_ref = s32[1,128]{1,0:T(1,128)} pad(s32[1,8]{1,0:T(1,128)} %param.25, s32[]{:T(128)} %constant.0.clone.1), padding=0_0x0_120 | pad | bytes 548 | tf_op jit(solution)/shard_map/jit(_pad)/pad | solution.py:352
  6.5 14.5 %open_rows.1 = (f32[3072,128]{1,0:T(8,128)}, f32[4608,128]{1,0:T(8,128)}, bf16[256,128]{1,0:T(8,128)(2,1)}, bf16[256,128]{1,0:T(8,128)(2,1)}, s32[4,1,128]{2,1,0:T(1,128)}) custom-call(s32[512]{0:T(512)} %bitcast.13, f32[45,3072]{1,0:T(8,128)} %height_ref.1, f32[3,3072]{1,0:T(4,128)} %coef_ref.1, f32[45,4608]{1,0:T(8,128)} %velocity_ref.1, f32[4608]{0:T(1024)} %edge_ref.1, ...), custom_call_target="tpu_custom_call" | custom-call | tf_op jit(solution)/shard_map/open_rows/pallas_call | solution.py:353
  21.0 30.8 %first_substep.1 = (f32[3072,128]{1,0:T(8,128)}, f32[4608,128]{1,0:T(8,128)}, bf16[512,128]{1,0:T(8,128)(2,1)}, bf16[480,1024]{1,0:T(8,128)(2,1)}, bf16[480,1024]{1,0:T(8,128)(2,1)}) custom-call(s32[9216]{0:T(1024)} %bitcast.8, s32[9216]{0:T(1024)} %bitcast.11, s32[512]{0:T(512)} %bitcast.14, s32[16]{0:T(128)} %bitcast.15, ...), custom_call_target="tpu_custom_call" | custom-call | tf_op jit(solution)/shard_map/first_substep/pallas_call | solution.py:381
  51.9 0.0 copy-done.1
  51.9 0.0 copy-done.4
  51.9 0.0 collective-permute-done.3.refs_7_
  51.9 0.0 copy-start.5
  51.9 0.0 collective-permute-done.2.refs_6_
  51.9 0.0 copy-start.3
  51.9 0.0 collective-permute-done.1.refs_5_
  51.9 0.0 copy-start.2
  52.0 0.0 collective-permute-done.refs_4_
  52.0 0.0 copy-start
  52.0 0.5 copy-done.5
  52.4 0.1 copy-done.3
  52.6 0.1 copy-done.2
  52.7 0.1 copy-done
  52.8 37.9 %second_substep.1 = (f32[45,3072]{1,0:T(8,128)}, f32[45,1024]{1,0:T(8,128)}, bf16[48,1024]{1,0:T(8,128)(2,1)}) custom-call(s32[9216]{0:T(1024)} %bitcast.9, s32[9216]{0:T(1024)} %bitcast.12, f32[3072,128]{1,0:T(8,128)} %get-tuple-element.23.h_ref, f32[4608,128]{1,0:T(8,128)} %get-tuple-element.24.v_ref, bf16[480,1024]{1,0:T(8,128)(2,1)} %get-tuple-element.25.x_own, ...), custom_call_target="tpu_custom_call" | custom-call | tf_op jit(solution)/shard_map/second_substep/pallas_call | solution.py:399
  90.7 2.3 %close_add.1 = f32[45,3072]{1,0:T(8,128)} custom-call(s32[16]{0:T(128)} %bitcast.16, s32[24]{0:T(128)} %bitcast.18, s32[4,8]{1,0:T(4,128)} %bitcast.17, f32[45,3072]{1,0:T(8,128)} %get-tuple-element.28.h_ref, f32[45,1024]{1,0:T(8,128)} %get-tuple-element.29.keep_ref, bf16[48,1024]{1,0:T(8,128)(2,1)} %get-tuple-element.30.got_ref), custom_call_target="tpu_custom_call" | custom-call | tf_op jit(solution)/shard_map/close_add/pallas_call | solution.py:418
Async XLA Ops:
  0.0 52.0 %collective-permute-start = (bf16[450,512]{1,0:T(8,128)(2,1)}, bf16[450,512]{1,0:T(8,128)(2,1)S(1)}, u32[]{:S(2)}, u32[]{:S(2)}) collective-permute-start(bf16[450,512]{1,0:T(8,128)(2,1)} %refs_0_.1), channel_id=1, source_target_pairs={{0,1},{1,0},{2,3},{3,2},{4,5},{5,4},{6,7},{7,6},{8,9},{9,8},{10,11... | collective-permute-start | bytes 1382408 | tf_op jit(solution)/shard_map/ppermute | solution.py:350
  0.5 51.5 %collective-permute-start.1 = (bf16[512,256]{1,0:T(8,128)(2,1)}, bf16[512,256]{1,0:T(8,128)(2,1)S(1)}, u32[]{:S(2)}, u32[]{:S(2)}) collective-permute-start(bf16[512,256]{1,0:T(8,128)(2,1)} %refs_1_.1), channel_id=1, source_target_pairs={{0,1},{1,0},{2,3},{3,2},{4,5},{5,4},{6,7},{7,6},{8,9},{9,8},{10,11... | collective-permute-start | bytes 786440 | tf_op jit(solution)/shard_map/ppermute | solution.py:350
  1.4 50.5 %copy-start.1 = (bf16[256,90]{1,0:T(8,128)(2,1)}, bf16[256,90]{1,0:T(8,128)(2,1)S(1)}, u32[]{:S(2)}) copy-start(bf16[256,90]{1,0:T(8,128)(2,1)S(1)} %copy.21.refs_2_) | copy-start | bytes 138244
  1.4 50.5 %collective-permute-start.2 = (bf16[256,90]{1,0:T(8,128)(2,1)S(1)}, bf16[256,90]{1,0:T(8,128)(2,1)S(1)}, u32[]{:S(2)}, u32[]{:S(2)}) collective-permute-start(bf16[256,90]{1,0:T(8,128)(2,1)S(1)} %copy.21.refs_2_), channel_id=1, source_target_pairs={{0,1},{1,0},{2,3},{3,2},{4,5},{5,4},{6,7},{7,6},{8,9},{9,8},{10,11... | collective-permute-start | bytes 138248 | tf_op jit(solution)/shard_map/ppermute | solution.py:350
  2.6 49.3 %copy-start.4 = (bf16[1,256]{1,0:T(2,128)(2,1)}, bf16[1,256]{1,0:T(2,128)(2,1)S(1)}, u32[]{:S(2)}) copy-start(bf16[1,256]{1,0:T(2,128)(2,1)S(1)} %broadcast_in_dim.7.refs_3_) | copy-start | bytes 1540
  2.6 49.3 %collective-permute-start.3 = (bf16[1,256]{1,0:T(2,128)(2,1)S(1)}, bf16[1,256]{1,0:T(2,128)(2,1)S(1)}, u32[]{:S(2)}, u32[]{:S(2)}) collective-permute-start(bf16[1,256]{1,0:T(2,128)(2,1)S(1)} %broadcast_in_dim.7.refs_3_), channel_id=1, source_target_pairs={{0,1},{1,0},{2,3},{3,2},{4,5},{5,4},{6,7},{7,6},{8,9},{9,8},{10,11... | collective-permute-start | bytes 1544 | tf_op jit(solution)/shard_map/ppermute | solution.py:350
  51.9 0.5 copy-start.5
  51.9 0.6 copy-start.3
  51.9 0.7 copy-start.2
  52.0 0.8 copy-start

commit v5 on v4

--- a/solution.py
+++ b/solution.py
@@ -282,7 +282,7 @@
     def silu(v):
         return (v / (1.0 + jnp.exp(-v))).astype(BF16)
 
-    chunk = 256
+    chunk = x_own.shape[1]
     levels = keep_ref.shape[0]
     ones = jnp.ones((1, chunk), BF16)
     for base in range(0, x_own.shape[1], chunk):

time: 93.4 us -> 91.4 us (0.979)
  Pallas kernels: 85.6 us -> 83.6 us
    pallas_call x1, Pallas kernels: 37.9 us -> 35.9 us  [body(): pl.pallas_call(functools.partial(second_kernel, (nq, pad, n_cells, n_role...]
  transfers between devices with their start and end apart: 4 -> 4, of which waited for: 0 -> 0; matrix products, arithmetic and copies ran while one was open for 6% -> 6% of each run, Pallas kernels for 49% -> 50%
where the time goes in v5:
time: 91.4 us; the launch traced here: 91.1 us
  Pallas kernels  83.6 us (91%)
  local copies, waits for them, and re-layouts  6.27 us (7%)
  starting transfers between devices  1.09 us (1%)
    pallas_call x1, Pallas kernels, body(): pl.pallas_call(functools.partial(second_kernel, (nq, pad, n_cells, n_role...  35.9 us
    pallas_call x1, Pallas kernels, body(): pl.pallas_call(functools.partial(first_kernel, levels), out_shape=(shape(...  30.8 us
    pallas_call x1, Pallas kernels, body(): pl.pallas_call(functools.partial(open_kernel, (n_cells, n_role)), out_sha...  14.5 us
    pallas_call x1, Pallas kernels, body(): pl.pallas_call(close_kernel, out_shape=shape((levels, cells), F32), in_sp...  2.31 us
  transfers between devices with their start and end apart: 4, of which 0 were waited for; matrix products, arithmetic and copies ran while one was open for 6% of the time, Pallas kernels for 50%

profile of v5, /device:TPU:0, one launch (start us, length us, event | category | flops | bytes accessed | tf_op | source)
XLA Modules:
  0.0 91.1 jit_solution(7051835202284689727)
XLA Ops:
  0.0 0.5 collective-permute-start
  0.5 0.1 collective-permute-start.1
  0.5 0.9 %copy.21.refs_2_ = bf16[256,90]{1,0:T(8,128)(2,1)S(1)} copy(bf16[256,90]{0,1:T(8,128)(2,1)} %param.31) | data formatting | bytes 92160 | tf_op args[15]
  1.4 0.0 copy-start.1
  1.4 0.5 collective-permute-start.2
  2.0 0.7 broadcast_in_dim.7.refs_3_
  2.6 0.0 copy-start.4
  2.6 0.1 collective-permute-start.3
  2.7 0.8 reshape.21
  3.5 0.6 copy.19
  4.1 1.3 %broadcast_in_dim.6.bias_one = bf16[1,512]{1,0:T(2,128)(2,1)} reshape(bf16[512]{0:T(512)(128)(2,1)} %param.28) | data formatting | bytes 2048 | tf_op jit(solution)/shard_map/broadcast_in_dim | solution.py:416
  5.4 1.2 %pad.4.recv_ref = s32[1,128]{1,0:T(1,128)} pad(s32[1,8]{1,0:T(1,128)} %param.25, s32[]{:T(128)} %constant.0.clone.1), padding=0_0x0_120 | pad | bytes 548 | tf_op jit(solution)/shard_map/jit(_pad)/pad | solution.py:352
  6.5 14.5 %open_rows.1 = (f32[3072,128]{1,0:T(8,128)}, f32[4608,128]{1,0:T(8,128)}, bf16[256,128]{1,0:T(8,128)(2,1)}, bf16[256,128]{1,0:T(8,128)(2,1)}, s32[4,1,128]{2,1,0:T(1,128)}) custom-call(s32[512]{0:T(512)} %bitcast.13, f32[45,3072]{1,0:T(8,128)} %height_ref.1, f32[3,3072]{1,0:T(4,128)} %coef_ref.1, f32[45,4608]{1,0:T(8,128)} %velocity_ref.1, f32[4608]{0:T(1024)} %edge_ref.1, ...), custom_call_target="tpu_custom_call" | custom-call | tf_op jit(solution)/shard_map/open_rows/pallas_call | solution.py:353
  21.0 30.8 %first_substep.1 = (f32[3072,128]{1,0:T(8,128)}, f32[4608,128]{1,0:T(8,128)}, bf16[512,128]{1,0:T(8,128)(2,1)}, bf16[480,1024]{1,0:T(8,128)(2,1)}, bf16[480,1024]{1,0:T(8,128)(2,1)}) custom-call(s32[9216]{0:T(1024)} %bitcast.8, s32[9216]{0:T(1024)} %bitcast.11, s32[512]{0:T(512)} %bitcast.14, s32[16]{0:T(128)} %bitcast.15, ...), custom_call_target="tpu_custom_call" | custom-call | tf_op jit(solution)/shard_map/first_substep/pallas_call | solution.py:381
  51.9 0.0 copy-done.1
  51.9 0.0 copy-done.4
  51.9 0.0 collective-permute-done.3.refs_7_
  51.9 0.0 copy-start.5
  51.9 0.0 collective-permute-done.2.refs_6_
  51.9 0.0 copy-start.3
  51.9 0.0 collective-permute-done.1.refs_5_
  51.9 0.0 copy-start.2
  52.0 0.0 collective-permute-done.refs_4_
  52.0 0.0 copy-start
  52.0 0.5 copy-done.5
  52.4 0.1 copy-done.3
  52.6 0.1 copy-done.2
  52.7 0.1 copy-done
  52.8 35.9 %second_substep.1 = (f32[45,3072]{1,0:T(8,128)}, f32[45,1024]{1,0:T(8,128)}, bf16[48,1024]{1,0:T(8,128)(2,1)}) custom-call(s32[9216]{0:T(1024)} %bitcast.9, s32[9216]{0:T(1024)} %bitcast.12, f32[3072,128]{1,0:T(8,128)} %get-tuple-element.23.h_ref, f32[4608,128]{1,0:T(8,128)} %get-tuple-element.24.v_ref, bf16[480,1024]{1,0:T(8,128)(2,1)} %get-tuple-element.25.x_own, ...), custom_call_target="tpu_custom_call" | custom-call | tf_op jit(solution)/shard_map/second_substep/pallas_call | solution.py:399
  88.7 2.3 %close_add.1 = f32[45,3072]{1,0:T(8,128)} custom-call(s32[16]{0:T(128)} %bitcast.16, s32[24]{0:T(128)} %bitcast.18, s32[4,8]{1,0:T(4,128)} %bitcast.17, f32[45,3072]{1,0:T(8,128)} %get-tuple-element.28.h_ref, f32[45,1024]{1,0:T(8,128)} %get-tuple-element.29.keep_ref, bf16[48,1024]{1,0:T(8,128)(2,1)} %get-tuple-element.30.got_ref), custom_call_target="tpu_custom_call" | custom-call | tf_op jit(solution)/shard_map/close_add/pallas_call | solution.py:418
Async XLA Ops:
  0.0 52.0 %collective-permute-start = (bf16[450,512]{1,0:T(8,128)(2,1)}, bf16[450,512]{1,0:T(8,128)(2,1)S(1)}, u32[]{:S(2)}, u32[]{:S(2)}) collective-permute-start(bf16[450,512]{1,0:T(8,128)(2,1)} %refs_0_.1), channel_id=1, source_target_pairs={{0,1},{1,0},{2,3},{3,2},{4,5},{5,4},{6,7},{7,6},{8,9},{9,8},{10,11... | collective-permute-start | bytes 1382408 | tf_op jit(solution)/shard_map/ppermute | solution.py:350
  0.5 51.5 %collective-permute-start.1 = (bf16[512,256]{1,0:T(8,128)(2,1)}, bf16[512,256]{1,0:T(8,128)(2,1)S(1)}, u32[]{:S(2)}, u32[]{:S(2)}) collective-permute-start(bf16[512,256]{1,0:T(8,128)(2,1)} %refs_1_.1), channel_id=1, source_target_pairs={{0,1},{1,0},{2,3},{3,2},{4,5},{5,4},{6,7},{7,6},{8,9},{9,8},{10,11... | collective-permute-start | bytes 786440 | tf_op jit(solution)/shard_map/ppermute | solution.py:350
  1.4 50.5 %copy-start.1 = (bf16[256,90]{1,0:T(8,128)(2,1)}, bf16[256,90]{1,0:T(8,128)(2,1)S(1)}, u32[]{:S(2)}) copy-start(bf16[256,90]{1,0:T(8,128)(2,1)S(1)} %copy.21.refs_2_) | copy-start | bytes 138244
  1.4 50.5 %collective-permute-start.2 = (bf16[256,90]{1,0:T(8,128)(2,1)S(1)}, bf16[256,90]{1,0:T(8,128)(2,1)S(1)}, u32[]{:S(2)}, u32[]{:S(2)}) collective-permute-start(bf16[256,90]{1,0:T(8,128)(2,1)S(1)} %copy.21.refs_2_), channel_id=1, source_target_pairs={{0,1},{1,0},{2,3},{3,2},{4,5},{5,4},{6,7},{7,6},{8,9},{9,8},{10,11... | collective-permute-start | bytes 138248 | tf_op jit(solution)/shard_map/ppermute | solution.py:350
  2.6 49.3 %copy-start.4 = (bf16[1,256]{1,0:T(2,128)(2,1)}, bf16[1,256]{1,0:T(2,128)(2,1)S(1)}, u32[]{:S(2)}) copy-start(bf16[1,256]{1,0:T(2,128)(2,1)S(1)} %broadcast_in_dim.7.refs_3_) | copy-start | bytes 1540
  2.6 49.3 %collective-permute-start.3 = (bf16[1,256]{1,0:T(2,128)(2,1)S(1)}, bf16[1,256]{1,0:T(2,128)(2,1)S(1)}, u32[]{:S(2)}, u32[]{:S(2)}) collective-permute-start(bf16[1,256]{1,0:T(2,128)(2,1)S(1)} %broadcast_in_dim.7.refs_3_), channel_id=1, source_target_pairs={{0,1},{1,0},{2,3},{3,2},{4,5},{5,4},{6,7},{7,6},{8,9},{9,8},{10,11... | collective-permute-start | bytes 1544 | tf_op jit(solution)/shard_map/ppermute | solution.py:350
  51.9 0.5 copy-start.5
  51.9 0.6 copy-start.3
  51.9 0.7 copy-start.2
  52.0 0.8 copy-start
